TPU v7x, 128 devices: a whole 4x4x4 slice. The times are simulated.
128 devices in a mesh: frame: 8 (over z_hi, x), patch: 16 (over y, z_lo, core).
Axes of the slice: x: 4, y: 4, z: 4 (z_hi: 2, z_lo: 2; z = z_hi * 2 + z_lo), core: 2. Of those that a mesh axis runs over, the one named last changes fastest.
Arguments:
- tokens: bfloat16 [32, 1536, 1152], P('frame', 'patch'), may hold values from -6 to 6
- modulation: float32 [2, 3, 1152], replicated, may hold values from -0.5 to 1
- spatial_input: bfloat16 [1152, 3456], replicated, may hold values from -4 to 4
- spatial_output: bfloat16 [1152, 1152], replicated, may hold values from -0.1875 to 0.1875
- temporal_input: bfloat16 [1152, 3456], replicated, may hold values from -4 to 4
- temporal_output: bfloat16 [1152, 1152], replicated, may hold values from -0.1875 to 0.1875
Outputs:
- result: bfloat16 [32, 1536, 1152], P('frame', 'patch')
All inputs are finite; a program needn't handle non-finite values.
Results may differ from a plain program's by a relative error of at most 0.03.
The roundings to bfloat16 on the way count: a program that leaves them out, or rounds other values in their place, can miss the bound.
Values may be sent and summed in bfloat16 or wider, within the bound.
A program may use at most 320 MiB of HBM per device.

v0:
```python
import math

import jax
import jax.numpy as jnp
from jax import lax
from jax.sharding import PartitionSpec as P

HEADS = 16
HEAD = 72


def modulate(values, table):
    wide = values.astype(jnp.float32)
    centre = jnp.mean(wide, axis=-1, keepdims=True)
    spread = jnp.mean(jnp.square(wide - centre), axis=-1, keepdims=True)
    normed = (wide - centre) * lax.rsqrt(spread + 1e-06)
    return (normed * (1.0 + table[1]) + table[0]).astype(jnp.bfloat16)


def project_in(mixed, weights):
    lead = mixed.shape[:-1]
    flat = jnp.dot(mixed.reshape(-1, mixed.shape[-1]), weights, preferred_element_type=jnp.float32)
    return flat.astype(jnp.bfloat16).reshape(lead + (3, HEADS, HEAD))


def softmax_rows(scores):
    top = jnp.max(scores, axis=-1, keepdims=True)
    expo = jnp.exp(scores - top)
    return (expo / jnp.sum(expo, axis=-1, keepdims=True)).astype(jnp.bfloat16)


def residual(values, attended, weights, table):
    flat = jnp.dot(
        attended.reshape(-1, weights.shape[0]), weights, preferred_element_type=jnp.float32
    )
    return (values.astype(jnp.float32) + table[2] * flat.reshape(values.shape)).astype(jnp.bfloat16)


def attend_batch(queries, keys, values):
    scores = jnp.einsum(
        "bqhe,bkhe->bhqk", queries, keys, preferred_element_type=jnp.float32
    ) / math.sqrt(HEAD)
    weights = softmax_rows(scores)
    mixed = jnp.einsum("bhqk,bkhe->bqhe", weights, values, preferred_element_type=jnp.float32)
    return mixed.astype(jnp.bfloat16)


def attend_frames(blocks):
    scores = jnp.einsum(
        "qphe,kphe->phqk", blocks[:, :, 0], blocks[:, :, 1], preferred_element_type=jnp.float32
    ) / math.sqrt(HEAD)
    weights = softmax_rows(scores)
    mixed = jnp.einsum(
        "phqk,kphe->qphe", weights, blocks[:, :, 2], preferred_element_type=jnp.float32
    )
    return mixed.astype(jnp.bfloat16)


def shards(tokens, modulation, spatial_input, spatial_output, temporal_input, temporal_output):
    packed = project_in(modulate(tokens, modulation[0]), spatial_input)
    keys_all, values_all = (
        lax.all_gather(packed[:, :, 1], "patch", axis=1, tiled=True),
        lax.all_gather(packed[:, :, 2], "patch", axis=1, tiled=True),
    )
    attended = attend_batch(packed[:, :, 0], keys_all, values_all)
    updated = residual(tokens, attended, spatial_output, modulation[0])
    modulated = modulate(updated, modulation[1])
    packed = project_in(modulated, temporal_input)
    spread_out = attend_frames(
        lax.all_to_all(packed, "frame", split_axis=1, concat_axis=0, tiled=True)
    )
    attended = lax.all_to_all(spread_out, "frame", split_axis=0, concat_axis=1, tiled=True)
    return residual(updated, attended, temporal_output, modulation[1])


def solution(mesh):
    in_specs = (P("frame", "patch", None), P(), P(), P(), P(), P())
    out_specs = P("frame", "patch", None)
    return jax.shard_map(shards, mesh=mesh, in_specs=in_specs, out_specs=out_specs, check_vma=False)
```

profile of v0, /device:TPU:0, one launch (start us, length us, event | category | flops | bytes accessed | tf_op | source)
XLA Modules:
  0.0 502.8 jit_solution(14325684555801463811)
XLA Ops:
  6.5 0.0 copy-start
  6.5 0.0 all-gather.7.cloned.1.call-start
  6.5 1.6 slice_reduce_fusion.1
  8.1 1.4 convert_reduce_fusion
  9.5 1.6 fusion.22
  11.1 1.6 fusion.25
  12.7 8.2 %convolution_convert_fusion.1 = bf16[384,3456]{1,0:T(8,128)(2,1)} fusion(bf16[384,1152]{1,0:T(8,128)(2,1)S(1)} %bitcast.61, bf16[1152,3456]{1,0:T(8,128)(2,1)} %param.8), kind=kOutput, calls=%fused_computation.12 | convolution fusion | flops 3058974720 | bytes 11501568 | tf_op jit(solution)/shard_map/dot_general | solution.py:22
  20.9 4.4 copy.47
  25.3 7.5 %reshape.62 = bf16[4,96,3,16,72]{1,0,4,3,2:T(4,128)(2,1)} reshape(bf16[384,3456]{0,1:T(8,128)(2,1)} %copy.47) | data formatting | bytes 5308416 | tf_op jit(solution)/shard_map/reshape | solution.py:23
  32.9 4.7 fusion.35
  37.5 4.5 copy.51
  42.0 0.0 all-gather.7.cloned.1.call-update
  42.1 0.2 all-gather.5.cloned.1.call-start
  42.3 4.5 copy.48
  46.8 0.0 all-gather.5.cloned.1.call-update
  46.8 129.1 %all-gather.7.cloned.1.call-done = bf16[4,1536,1,16,72]{4,3,2,0,1:T(8,128)(2,1)} async-done(((bf16[4,96,1,16,72]{4,3,2,0,1:T(8,128)(2,1)}), bf16[4,1536,1,16,72]{4,3,2,0,1:T(8,128)(2,1)}) %all-gather.7.cloned.1.call-update) | async-done | bytes 14155792 | tf_op jit(solution)/shard_map/all_gather | solution.py:62
  175.9 29.9 %copy.52 = bf16[4,1536,1,16,72]{1,4,3,0,2:T(8,128)(2,1)} copy(bf16[4,1536,1,16,72]{4,3,2,0,1:T(8,128)(2,1)} %all-gather.7.cloned.1.call-done) | data formatting | bytes 28311552 | tf_op jit(solution)/shard_map/all_gather | solution.py:62
  205.8 19.0 %fusion.7 = f32[4,16,96,1536]{3,2,1,0:T(8,128)} fusion(bf16[4,1536,1,16,72]{1,4,3,0,2:T(8,128)(2,1)} %copy.52, bf16[4,96,1,16,72]{1,0,4,3,2:T(4,128)(2,1)} %get-tuple-element.13), kind=kOutput, calls=%fused_computation.8 | convolution fusion | flops 1358954496 | bytes 52789248 | tf_op jit(solution)/shard_map/bqhe,bkhe->bhqk/dot_general | solution.py:40
  224.7 42.9 %fusion.36 = (f32[4,16,96]{2,1,0:T(8,128)}, f32[4,16,96,1536]{3,2,1,0:T(8,128)}) fusion(f32[4,16,96,1536]{3,2,1,0:T(8,128)} %fusion.7), kind=kOutput, calls=%fused_computation.60 | output fusion | flops 37750272 | bytes 75522048 | tf_op jit(solution)/shard_map/sub | solution.py:28
  267.6 41.8 %all-gather.5.cloned.1.call-done = bf16[4,1536,1,16,72]{4,3,2,0,1:T(8,128)(2,1)} async-done(((bf16[4,96,1,16,72]{4,3,2,0,1:T(8,128)(2,1)}), bf16[4,1536,1,16,72]{4,3,2,0,1:T(8,128)(2,1)}) %all-gather.5.cloned.1.call-update) | async-done | bytes 14155792 | tf_op jit(solution)/shard_map/all_gather | solution.py:63
  309.5 29.6 %copy.49 = bf16[4,1536,1,16,72]{1,4,3,0,2:T(8,128)(2,1)} copy(bf16[4,1536,1,16,72]{4,3,2,0,1:T(8,128)(2,1)} %all-gather.5.cloned.1.call-done) | data formatting | bytes 28311552 | tf_op jit(solution)/shard_map/all_gather | solution.py:63
  339.0 0.0 copy-start.2
  339.0 19.7 %fusion.29 = bf16[4,16,72,96]{3,2,1,0:T(8,128)(2,1)} fusion(f32[4,16,96,1536]{3,2,1,0:T(8,128)} %get-tuple-element.15, f32[4,16,96]{2,1,0:T(8,128)} %get-tuple-element.14, bf16[4,1536,1,16,72]{1,4,3,0,2:T(8,128)(2,1)} %copy.49), kind=kOutput, calls=%fused_computation.44 | convolution fusion | flops 1378271232 | bytes 52813824 | tf_op jit(solution)/shard_map/bhqk,bkhe->bqhe/dot_general | solution.py:44
  358.7 0.0 copy-done
  358.7 0.0 copy-done.2
  358.7 2.9 fusion.37
  361.7 0.0 copy-start.1
  361.7 0.3 multiply_reduce_fusion.2
  362.0 0.9 copy-done.1
  363.0 0.4 add_convert_fusion
  363.3 8.5 %convolution_convert_fusion = bf16[384,3456]{1,0:T(8,128)(2,1)} fusion(bf16[384,1152]{1,0:T(8,128)(2,1)S(1)} %bitcast.62, bf16[1152,3456]{1,0:T(8,128)(2,1)} %param.10), kind=kOutput, calls=%fused_computation.11 | convolution fusion | flops 3058974720 | bytes 11501568 | tf_op jit(solution)/shard_map/dot_general | solution.py:22
  371.8 10.7 %reshape.69 = bf16[4,96,3,16,72]{4,3,2,1,0:T(8,128)(2,1)} reshape(bf16[384,3456]{1,0:T(8,128)(2,1)} %convolution_convert_fusion) | data formatting | bytes 5308416 | tf_op jit(solution)/shard_map/reshape | solution.py:23
  382.5 3.8 copy.55
  386.4 63.3 %all_to_all.33 = bf16[4,96,3,16,72]{4,3,2,0,1:T(8,128)(2,1)S(1)} all-to-all(bf16[4,96,3,16,72]{4,3,2,0,1:T(8,128)(2,1)S(1)} %copy.55), channel_id=1, replica_groups=mesh['frame'=8,'patch'=16] {'frame'}, dimensions={1} | all-to-all | bytes 5308416 | tf_op jit(solution)/shard_map/all_to_all | solution.py:70
  449.6 2.4 copy.57
  452.1 0.9 fusion.26
  453.0 7.2 %fusion.38 = (f32[12,16,32]{2,1,0:T(8,128)S(1)}, f32[12,16,32,32]{2,3,1,0:T(8,128)S(1)}) fusion(f32[12,16,32,32]{2,3,1,0:T(8,128)S(1)} %fusion.26), kind=kOutput, calls=%fused_computation.62 | output fusion | flops 786463 | bytes 1597440 | tf_op jit(solution)/shard_map/sub | solution.py:28
  460.2 0.7 fusion.32
  460.9 0.6 copy.59
  461.5 25.4 %all_to_all.34 = bf16[32,12,16,72]{3,2,1,0:T(8,128)(2,1)S(1)} all-to-all(bf16[32,12,16,72]{3,2,1,0:T(8,128)(2,1)S(1)} %copy.59), channel_id=1, replica_groups=mesh['frame'=8,'patch'=16] {'frame'}, dimensions={0} | all-to-all | bytes 1769472 | tf_op jit(solution)/shard_map/all_to_all | solution.py:72
  486.9 0.0 copy-start.3
  486.9 1.4 copy.70
  488.4 3.0 dot_general.36
  491.4 0.0 copy-done.3
  491.4 4.6 fusion.12
  (4 shorter events, 0.0 us)
Async XLA Ops:
  6.5 352.2 %copy-start = (bf16[1152,1152]{1,0:T(8,128)(2,1)S(1)}, bf16[1152,1152]{1,0:T(8,128)(2,1)}, u32[]{:S(2)}) copy-start(bf16[1152,1152]{1,0:T(8,128)(2,1)} %param.9) | copy-start | bytes 7962628
  6.5 169.3 %all-gather.7.cloned.1.call-start = ((), (), s32[]{:S(2)}) async-start(), calls=%async_computation.3 | async-start | bytes 26738688 | tf_op jit(solution)/shard_map/all_gather | solution.py:62
  42.1 267.4 %all-gather.5.cloned.1.call-start = ((), (), s32[]{:S(2)}) async-start(), calls=%async_computation.2 | async-start | bytes 26738688 | tf_op jit(solution)/shard_map/all_gather | solution.py:63
  339.0 19.7 %copy-start.2 = (bf16[4,96,1152]{2,1,0:T(8,128)(2,1)S(1)}, bf16[4,96,1152]{2,1,0:T(8,128)(2,1)}, u32[]{:S(2)}) copy-start(bf16[4,96,1152]{2,1,0:T(8,128)(2,1)} %param.6) | copy-start | bytes 2654212
  361.7 1.3 copy-start.1
  486.9 4.5 copy-start.3
Sparse Core Ops, SparseCore 0:
  42.2 133.6 all-gather.6
  177.6 131.8 all-gather.4
where the time goes:
time: 505 us; the launch traced here: 503 us
  waiting for transfers between devices  171 us (34%)
  local copies, waits for them, and re-layouts  108 us (21%)
  blocking collectives  88.7 us (18%)
  matrix products  64.6 us (13%)
  other arithmetic  56.8 us (11%)
  between operations  13.5 us (3%)
    all_gather x1, waiting for transfers between devices, shards(): lax.all_gather(packed[:, :, 1], 'patch', axis=1, tiled=True)  129 us
    all_to_all x1, blocking collectives, shards(): lax.all_to_all(packed, 'frame', split_axis=1, concat_axis=0, tiled=True)  63.3 us
    sub x2, other arithmetic, softmax_rows(): expo = jnp.exp(scores - top)  50 us
    all_gather x1, waiting for transfers between devices, shards(): lax.all_gather(packed[:, :, 2], 'patch', axis=1, tiled=True)  41.8 us
    all_gather x1, local copies, waits for them, and re-layouts, shards(): lax.all_gather(packed[:, :, 1], 'patch', axis=1, tiled=True)  29.9 us
    all_gather x1, local copies, waits for them, and re-layouts, shards(): lax.all_gather(packed[:, :, 2], 'patch', axis=1, tiled=True)  29.6 us
    all_to_all x1, blocking collectives, shards(): lax.all_to_all(spread_out, 'frame', split_axis=0, concat_axis=1, tiled=True)  25.4 us
    reshape x3, local copies, waits for them, and re-layouts, project_in(): return flat.astype(jnp.bfloat16).reshape(lead + (3, HEADS, HEAD))  22.1 us
  transfers between devices with their start and end apart: 2, of which 2 were waited for; matrix products, arithmetic and copies ran while one was open for 19% of the time, Pallas kernels for 0%

commit v1 on v0

v1 whole, which is shorter than its diff:
```python
import functools
import math

import jax
import jax.numpy as jnp
from jax import lax
from jax.experimental import pallas as pl
from jax.experimental.pallas import tpu as pltpu
from jax.sharding import PartitionSpec as P

D = 1152
HEADS = 16
HEAD = 72
WIN = 640
SCALE = math.log2(math.e) / math.sqrt(HEAD)
MESH = pl.DeviceIdType.MESH
VMEM_LIMIT = 60 * 1024 * 1024
ORDER = (0, 1, 3, 2)


def modulate(values, table):
    wide = values.astype(jnp.float32)
    centre = jnp.mean(wide, axis=-1, keepdims=True)
    wide = wide - centre
    spread = jnp.mean(jnp.square(wide), axis=-1, keepdims=True)
    normed = wide * lax.rsqrt(spread + 1e-06)
    return (normed * (1.0 + table[1:2]) + table[0:1]).astype(jnp.bfloat16)


def nt_dot(a, b):
    return lax.dot_general(a, b, (((1,), (1,)), ((), ())), preferred_element_type=jnp.float32)


def nn_dot(a, b):
    return jnp.dot(a, b, preferred_element_type=jnp.float32)


def head_attention(queries, keys, values, start, free, bias=None):
    lane = lax.broadcasted_iota(jnp.int32, (1, 256), 1)
    mine = (lane >= start) & (lane < start + HEAD)
    one = jnp.where(lane == free, 1.0, 0.0)
    chosen = queries * jnp.where(mine, 1.0, 0.0).astype(jnp.bfloat16)
    counted = values * (1.0 - one).astype(jnp.bfloat16) + one.astype(jnp.bfloat16)
    scores = nt_dot(chosen, keys)
    if bias is not None:
        scores = scores + bias
    top = jnp.max(scores, axis=-1, keepdims=True)
    weights = jnp.exp2(scores - top).astype(jnp.bfloat16)
    mixed = nn_dot(weights, counted)
    mixed = mixed * (1.0 / mixed[:, free : free + 1])
    return jnp.where(mine, mixed, 0.0)


def spatial_kernel(
    tok, mod, w_in, w_out, out,
    x, w, wo, q, k, v, att, att_in, u,
    load_sem, y_send, y_recv, s_send, s_recv, z_send, z_recv, a_send, a_recv, r_send, r_recv, o_sem,
):
    frame = lax.axis_index("frame")
    patch = lax.axis_index("patch")
    y = patch // 4
    z = (patch // 2) % 2
    core = patch % 2
    sibling = (frame, y * 4 + z * 2 + (1 - core))
    across = (frame, y * 4 + (1 - z) * 2 + core)

    def along(step):
        return (frame, ((y + step) % 4) * 4 + z * 2 + core)

    loads = [pltpu.make_async_copy(tok.at[y], x.at[0, 0, 0], load_sem.at[0])]
    for part in range(3):
        columns = pl.ds(pl.multiple_of(part * D + core * 512, 128), WIN)
        loads.append(
            pltpu.make_async_copy(w_in.at[:, columns], w.at[:, pl.ds(part * WIN, WIN)], load_sem.at[1 + part])
        )
    loads.append(pltpu.make_async_copy(w_out, wo, load_sem.at[4]))
    for load in loads:
        load.start()

    barrier = pltpu.get_barrier_semaphore()
    for peer in (sibling, across, along(1), along(2), along(3)):
        pl.semaphore_signal(barrier, inc=1, device_id=peer, device_id_type=MESH)
    pl.semaphore_wait(barrier, 5)

    def remote(src, dst, send, recv, peer):
        return pltpu.make_async_remote_copy(
            src_ref=src, dst_ref=dst, send_sem=send, recv_sem=recv, device_id=peer, device_id_type=MESH
        )

    along_y = {}
    for d in (1, 3, 2):
        along_y[d] = remote(tok.at[(y + 4 - d) % 4], x.at[0, d, 0], y_send.at[d], y_recv.at[d], along(4 - d))
        along_y[d].start()
    loads[0].wait()

    to_sibling = {}
    over_z = {}

    def pass_on(d):
        over_z[d] = remote(x.at[0, d, 0], x.at[1, d, 0], z_send.at[d], z_recv.at[d], across)
        over_z[d].start()
        to_sibling[0, d] = remote(x.at[0, d, 0], x.at[0, d, 1], s_send.at[0, d], s_recv.at[0, d], sibling)
        to_sibling[0, d].start()

    def pass_z(d):
        over_z[d].wait_recv()
        to_sibling[1, d] = remote(x.at[1, d, 0], x.at[1, d, 1], s_send.at[1, d], s_recv.at[1, d], sibling)
        to_sibling[1, d].start()

    table = mod[0]

    def project(half, d):
        mixed = modulate(x[half, d].reshape(192, D), table)
        rows = pl.ds((half * 4 + d) * 192, 192)
        if half == 0:
            q[pl.ds(d * 192, 192), :] = (nn_dot(mixed, w[:, :WIN]) * SCALE).astype(jnp.bfloat16)
        k[rows, :] = nn_dot(mixed, w[:, WIN : 2 * WIN]).astype(jnp.bfloat16)
        v[rows, :] = nn_dot(mixed, w[:, 2 * WIN :]).astype(jnp.bfloat16)

    for step, d in enumerate(ORDER):
        if d:
            along_y[d].wait_recv()
        pass_on(d)
        to_sibling[0, d].wait_recv()
        if step == 0:
            for load in loads[1:4]:
                load.wait()
        project(0, d)
    for d in ORDER:
        pass_z(d)
        to_sibling[1, d].wait_recv()
        project(1, d)
    loads[4].wait()

    def attend(d):
        rows = pl.ds(d * 192, 192)
        carry = jnp.zeros((192, 128), jnp.float32)
        for j in range(4):
            window = slice(128 * j, 128 * j + 256)
            queries, keys, values = q[rows, window], k[:, window], v[:, window]
            both = head_attention(queries, keys, values, 16 * j + 64 * core, 255)
            both = both + head_attention(queries, keys, values, 16 * j + 72 + 64 * core, 0)
            att[d, :, 128 * j : 128 * j + 128] = (carry + both[:, :128]).astype(jnp.bfloat16)
            carry = both[:, 128:]
        att[d, :, 512:] = carry.astype(jnp.bfloat16)
        swap(d).start()

    def swap(d):
        return remote(att.at[d, pl.ds(96, 96)], att_in.at[d], a_send.at[d], a_recv.at[d], sibling)

    def give_back(d):
        return remote(u.at[d], out.at[y], r_send.at[d], r_recv.at[d], along(d))

    def finish(d):
        swap(d).wait_recv()
        mine = pl.ds(pl.multiple_of(core * 512, 128), WIN)
        other = pl.ds(pl.multiple_of((1 - core) * 512, 128), WIN)
        flat = nn_dot(att[d, :96], wo[mine, :]) + nn_dot(att_in[d], wo[other, :])
        u[d] = (x[0, d, 0].astype(jnp.float32) + table[2:3] * flat).astype(jnp.bfloat16)

    attend(1)

    def turn(d, carry):
        attend(d)
        finish(d - 1)
        give_back(d - 1).start()
        return carry

    lax.fori_loop(2, 4, turn, 0)
    attend(0)
    finish(3)
    give_back(3).start()
    finish(0)
    own = pltpu.make_async_copy(u.at[0], out.at[y], o_sem)
    own.start()

    for d in (1, 2, 3):
        landed = remote(u.at[d], out.at[(y + 4 - d) % 4], r_send.at[d], r_recv.at[d], along(d))
        landed.wait_recv()
        give_back(d).wait_send()
        along_y[d].wait_send()
    for d in range(4):
        swap(d).wait_send()
        over_z[d].wait_send()
        to_sibling[0, d].wait_send()
        to_sibling[1, d].wait_send()
    own.wait()


def spatial(tokens, modulation, w_in, w_out):
    dma = pltpu.SemaphoreType.DMA
    any_space = pl.BlockSpec(memory_space=pl.ANY)
    return pl.pallas_call(
        spatial_kernel,
        out_shape=jax.ShapeDtypeStruct((4, 96, D), jnp.bfloat16),
        in_specs=[any_space, pl.BlockSpec(memory_space=pltpu.VMEM), any_space, any_space],
        out_specs=any_space,
        scratch_shapes=[
            pltpu.VMEM((2, 4, 2, 96, D), jnp.bfloat16),
            pltpu.VMEM((D, 3 * WIN), jnp.bfloat16),
            pltpu.VMEM((D, D), jnp.bfloat16),
            pltpu.VMEM((768, WIN), jnp.bfloat16),
            pltpu.VMEM((1536, WIN), jnp.bfloat16),
            pltpu.VMEM((1536, WIN), jnp.bfloat16),
            pltpu.VMEM((4, 192, WIN), jnp.bfloat16),
            pltpu.VMEM((4, 96, WIN), jnp.bfloat16),
            pltpu.VMEM((4, 96, D), jnp.bfloat16),
            dma((5,)),
            dma((4,)), dma((4,)),
            dma((2, 4)), dma((2, 4)),
            dma((4,)), dma((4,)),
            dma((4,)), dma((4,)),
            dma((4,)), dma((4,)),
            dma,
        ],
        compiler_params=pltpu.CompilerParams(
            collective_id=0, has_side_effects=True, vmem_limit_bytes=VMEM_LIMIT
        ),
        name="spatial_block",
    )(tokens, modulation, w_in, w_out)


def shuffle(rows_to, forward):
    a = lax.broadcasted_iota(jnp.int32, (384, 384), 0)
    b = lax.broadcasted_iota(jnp.int32, (384, 384), 1)
    grouped, plain = (a, b) if forward else (b, a)
    source = ((grouped // 4) % 4) * 96 + (grouped // 16) * 4 + grouped % 4
    return jnp.where(source == plain, 1.0, 0.0).astype(jnp.bfloat16)


def temporal_kernel(
    upd, mod, w_in, w_out, out,
    w, wo, g, t, packed, att, r, back,
    load_sem, g_send, g_recv, r_send, r_recv, own_sem,
):
    frame = lax.axis_index("frame")
    patch = lax.axis_index("patch")
    loads = [pltpu.make_async_copy(w_in, w, load_sem.at[0]), pltpu.make_async_copy(w_out, wo, load_sem.at[1])]
    for load in loads:
        load.start()

    def peer(step):
        return ((frame + step) % 8, patch)

    barrier = pltpu.get_barrier_semaphore()
    for step in range(1, 8):
        pl.semaphore_signal(barrier, inc=1, device_id=peer(step), device_id_type=MESH)

    g[...] = nn_dot(shuffle(384, True), upd[...].reshape(384, D)).astype(jnp.bfloat16).reshape(8, 3, 16, D)
    pl.semaphore_wait(barrier, 7)

    def remote(src, dst, send, recv, device):
        return pltpu.make_async_remote_copy(
            src_ref=src, dst_ref=dst, send_sem=send, recv_sem=recv, device_id=device, device_id_type=MESH
        )

    def spread(step):
        return remote(g.at[(frame + step) % 8], t.at[:, frame], g_send.at[step], g_recv.at[step], peer(step))

    def spread_in(step):
        return remote(g.at[0], t.at[:, (frame + 8 - step) % 8], g_send.at[step], g_recv.at[step], peer(step))

    def collect(step):
        return remote(r.at[:, (frame + step) % 8], back.at[frame], r_send.at[step], r_recv.at[step], peer(step))

    def collect_in(step):
        return remote(r.at[:, 0], back.at[(frame + 8 - step) % 8], r_send.at[step], r_recv.at[step], peer(step))

    for step in range(1, 8):
        spread(step).start()
    own = pltpu.make_async_copy(g.at[frame], t.at[:, frame], own_sem.at[0])
    own.start()
    own.wait()
    for step in range(1, 8):
        spread_in(step).wait_recv()

    table = mod[1]
    loads[0].wait()
    mixed = modulate(t[...].reshape(384, D), table)
    packed[:, :D] = (nn_dot(mixed, w[:, :D]) * SCALE).astype(jnp.bfloat16)
    packed[:, D : 2 * D] = nn_dot(mixed, w[:, D : 2 * D]).astype(jnp.bfloat16)
    packed[:, 2 * D :] = nn_dot(mixed, w[:, 2 * D :]).astype(jnp.bfloat16)

    a = lax.broadcasted_iota(jnp.int32, (128, 128), 0)
    b = lax.broadcasted_iota(jnp.int32, (128, 128), 1)
    bias = jnp.where(a % 4 == b % 4, 0.0, -1e30)

    def attend(group, carry):
        rows = pl.ds(pl.multiple_of(group * 128, 128), 128)
        tiles = {}
        for h in range(HEADS):
            tile = min(HEAD * h // 128, 7)
            start = HEAD * h - 128 * tile
            at = 128 * tile
            mixed = head_attention(
                packed[rows, at : at + 256],
                packed[rows, D + at : D + at + 256],
                packed[rows, 2 * D + at : 2 * D + at + 256],
                start, 0 if start else 255, bias,
            )
            for side in range(2):
                piece = mixed[:, 128 * side : 128 * side + 128]
                tiles[tile + side] = tiles[tile + side] + piece if tile + side in tiles else piece
        for tile in range(9):
            att[rows, 128 * tile : 128 * tile + 128] = tiles[tile].astype(jnp.bfloat16)
        return carry

    lax.fori_loop(0, 3, attend, 0)
    loads[1].wait()
    flat = nn_dot(att[...], wo[...])
    r[...] = (
        (t[...].reshape(384, D).astype(jnp.float32) + table[2:3] * flat).astype(jnp.bfloat16).reshape(3, 8, 16, D)
    )
    for step in range(1, 8):
        collect(step).start()
    own = pltpu.make_async_copy(r.at[:, frame], back.at[frame], own_sem.at[1])
    own.start()
    own.wait()
    for step in range(1, 8):
        collect_in(step).wait_recv()
    out[...] = nn_dot(shuffle(384, False), back[...].reshape(384, D)).astype(jnp.bfloat16).reshape(4, 96, D)
    for step in range(1, 8):
        spread(step).wait_send()
        collect(step).wait_send()


def temporal(updated, modulation, w_in, w_out):
    dma = pltpu.SemaphoreType.DMA
    any_space = pl.BlockSpec(memory_space=pl.ANY)
    vmem = pl.BlockSpec(memory_space=pltpu.VMEM)
    return pl.pallas_call(
        temporal_kernel,
        out_shape=jax.ShapeDtypeStruct((4, 96, D), jnp.bfloat16),
        in_specs=[vmem, vmem, any_space, any_space],
        out_specs=vmem,
        scratch_shapes=[
            pltpu.VMEM((D, 3 * D), jnp.bfloat16),
            pltpu.VMEM((D, D), jnp.bfloat16),
            pltpu.VMEM((8, 3, 16, D), jnp.bfloat16),
            pltpu.VMEM((3, 8, 16, D), jnp.bfloat16),
            pltpu.VMEM((384, 3 * D), jnp.bfloat16),
            pltpu.VMEM((384, D), jnp.bfloat16),
            pltpu.VMEM((3, 8, 16, D), jnp.bfloat16),
            pltpu.VMEM((8, 3, 16, D), jnp.bfloat16),
            dma((2,)),
            dma((8,)), dma((8,)),
            dma((8,)), dma((8,)),
            dma((2,)),
        ],
        compiler_params=pltpu.CompilerParams(
            collective_id=1, has_side_effects=True, vmem_limit_bytes=VMEM_LIMIT
        ),
        name="temporal_block",
    )(updated, modulation, w_in, w_out)


def shards(tokens, modulation, spatial_input, spatial_output, temporal_input, temporal_output):
    updated = spatial(tokens, modulation, spatial_input, spatial_output)
    return temporal(updated, modulation, temporal_input, temporal_output)


def solution(mesh):
    in_specs = (P("frame", "patch", None), P(), P(), P(), P(), P())
    out_specs = P("frame", "patch", None)
    return jax.shard_map(shards, mesh=mesh, in_specs=in_specs, out_specs=out_specs, check_vma=False)
```

time: 505 us -> 111 us (0.22)
  waiting for transfers between devices: 171 us -> 0 us
  Pallas kernels: 0 us -> 106 us
  local copies, waits for them, and re-layouts: 108 us -> 3.52 us
  blocking collectives: 88.7 us -> 0 us
  matrix products: 64.6 us -> 0 us
  other arithmetic: 56.8 us -> 0 us
  between operations: 13.5 us -> 0.02 us
    all_gather x2 -> x0, waiting for transfers between devices: 171 us -> none  [the longest x1 129 us: shards(): lax.all_gather(packed[:, :, 1], 'patch', axis=1, tiled=True)]
    pallas_call x0 -> x2, Pallas kernels: none -> 106 us  [the longest x1 58.3 us: spatial(): pl.pallas_call(spatial_kernel, out_shape=jax.ShapeDtypeStruct((4, 96, D),...]
    all_to_all x2 -> x0, blocking collectives: 88.7 us -> none  [the longest x1 63.3 us: shards(): lax.all_to_all(packed, 'frame', split_axis=1, concat_axis=0, tiled=True)]
    dot_general x8 -> x0, matrix products: 64.6 us -> none  [the longest x1 19.7 us: attend_batch(): jnp.einsum('bhqk,bkhe->bqhe', weights, values, preferred_element_type=jnp...]
    all_gather x2 -> x0, local copies, waits for them, and re-layouts: 59.5 us -> none  [the longest x1 29.9 us: shards(): lax.all_gather(packed[:, :, 1], 'patch', axis=1, tiled=True)]
    sub x2 -> x0, other arithmetic: 50 us -> none  [softmax_rows(): expo = jnp.exp(scores - top)]
    reshape x3 -> x0, local copies, waits for them, and re-layouts: 22.1 us -> none  [project_in(): return flat.astype(jnp.bfloat16).reshape(lead + (3, HEADS, HEAD))]
    slice x3 -> x0, local copies, waits for them, and re-layouts: 13.6 us -> none  [the longest x2 9.15 us: shards(): packed[:, :, 2]]
  transfers between devices with their start and end apart: 2 -> 0, of which waited for: 2 -> 0; matrix products, arithmetic and copies ran while one was open for 19% -> 0% of each run, Pallas kernels for 0% -> 0%
where the time goes in v1:
time: 111 us; the launch traced here: 109 us
  Pallas kernels  106 us (95%)
  local copies, waits for them, and re-layouts  3.52 us (3%)
    pallas_call x1, Pallas kernels, spatial(): pl.pallas_call(spatial_kernel, out_shape=jax.ShapeDtypeStruct((4, 96, D),...  58.3 us
    pallas_call x1, Pallas kernels, temporal(): pl.pallas_call(temporal_kernel, out_shape=jax.ShapeDtypeStruct((4, 96, D)...  47.5 us
    unnamed x2, local copies, waits for them, and re-layouts  3.52 us

profile of v1, /device:TPU:0, one launch (start us, length us, event | category | flops | bytes accessed | tf_op | source)
XLA Modules:
  0.0 109.3 jit_solution(10443976100503062746)
XLA Ops:
  0.0 1.4 %copy.7.mod = f32[2,3,1152]{2,1,0:T(4,128)} copy(f32[2,3,1152]{2,0,1:T(2,128)} %param.7) | data formatting | bytes 55296 | tf_op args[1]
  1.4 58.3 %spatial_block.1.upd = bf16[4,96,1152]{2,1,0:T(8,128)(2,1)} custom-call(bf16[4,96,1152]{2,1,0:T(8,128)(2,1)} %tok.1, f32[2,3,1152]{2,1,0:T(4,128)} %copy.7.mod, bf16[1152,3456]{1,0:T(8,128)(2,1)} %w_in.2, bf16[1152,1152]{1,0:T(8,128)(2,1)} %w_out.2), custom_call_target="tpu_custom_call" | custom-call | tf_op jit(solution)/shard_map/spatial_block/pallas_call | solution.py:193
  59.6 47.5 %temporal_block.1 = bf16[4,96,1152]{2,1,0:T(8,128)(2,1)} custom-call(bf16[4,96,1152]{2,1,0:T(8,128)(2,1)} %spatial_block.1.upd, f32[2,3,1152]{2,1,0:T(4,128)} %copy.7.mod, bf16[1152,3456]{1,0:T(8,128)(2,1)} %w_in.3, bf16[1152,1152]{1,0:T(8,128)(2,1)} %w_out.3), custom_call_target="tpu_custom_call" | custom-call | tf_op jit(solution)/shard_map/temporal_block/pallas_call | solution.py:331
  107.1 2.1 %copy.10 = bf16[4,96,1152]{2,1,0:T(8,128)(2,1)} copy(bf16[4,96,1152]{2,1,0:T(8,128)(2,1)} %temporal_block.1) | data formatting | bytes 1769472

commit v2 on v0

v2 whole, which is shorter than its diff:
```python
import math

import jax
import jax.numpy as jnp
from jax import lax
from jax.experimental import pallas as pl
from jax.experimental.pallas import tpu as pltpu
from jax.sharding import PartitionSpec as P

D = 1152
HEADS = 16
HEAD = 72
WIN = 640
EARLY = 960
SCALE = math.log2(math.e) / math.sqrt(HEAD)
MESH = pl.DeviceIdType.MESH
VMEM_LIMIT = 60 * 1024 * 1024
STEPS = (0, 1, 3, 2)


def modulate(values, table):
    wide = values.astype(jnp.float32)
    centre = jnp.mean(wide, axis=-1, keepdims=True)
    wide = wide - centre
    spread = jnp.mean(jnp.square(wide), axis=-1, keepdims=True)
    normed = wide * lax.rsqrt(spread + 1e-06)
    return (normed * (1.0 + table[1]) + table[0]).astype(jnp.bfloat16)


def nt_dot(a, b):
    return lax.dot_general(a, b, (((1,), (1,)), ((), ())), preferred_element_type=jnp.float32)


def nn_dot(a, b):
    return jnp.dot(a, b, preferred_element_type=jnp.float32)


def lanes(width):
    return lax.broadcasted_iota(jnp.int32, (1, width), 1)


def head_lanes(start):
    return (lanes(256) >= start) & (lanes(256) < start + HEAD)


def choose(queries, mine):
    return queries * jnp.where(mine, 1.0, 0.0).astype(jnp.bfloat16)


def count_in(values, free):
    one = jnp.where(lanes(256) == free, 1.0, 0.0)
    return values * (1.0 - one).astype(jnp.bfloat16) + one.astype(jnp.bfloat16)


def shuffle(forward):
    a = lax.broadcasted_iota(jnp.int32, (128, 128), 0)
    b = lax.broadcasted_iota(jnp.int32, (128, 128), 1)
    grouped, plain = (a, b) if forward else (b, a)
    source = ((grouped // 4) % 4) * 32 + (grouped // 16) * 4 + grouped % 4
    return jnp.where(source == plain, 1.0, 0.0).astype(jnp.bfloat16)


def kernel(
    tok, mod, w_in0, w_out0, w_in1, w_out1, out,
    x, w, wo, q, k, v, first, stat, att, att_in, u, gathered,
    wt, wto, grouped, t, packed, mixed_t, r, back, res,
    load_sem, y_send, y_recv, s_send, s_recv, z_send, z_recv, a_send, a_recv,
    u_send, u_recv, g_send, g_recv, r_send, r_recv, own_sem, o_sem,
):
    frame = lax.axis_index("frame")
    patch = lax.axis_index("patch")
    y = patch // 4
    z = (patch // 2) % 2
    core = patch % 2
    sibling = (frame, y * 4 + z * 2 + (1 - core))
    across = (frame, y * 4 + (1 - z) * 2 + core)

    def along(step):
        return (frame, ((y + step) % 4) * 4 + z * 2 + core)

    def peer(step):
        return ((frame + step) % 8, patch)

    loads = [pltpu.make_async_copy(tok.at[y], x.at[0, 0, 0], load_sem.at[0])]
    for part in range(3):
        columns = pl.ds(pl.multiple_of(part * D + core * 512, 128), WIN)
        loads.append(
            pltpu.make_async_copy(w_in0.at[:, columns], w.at[:, pl.ds(part * WIN, WIN)], load_sem.at[1 + part])
        )
    loads.append(pltpu.make_async_copy(w_out0, wo, load_sem.at[4]))
    loads.append(pltpu.make_async_copy(w_in1, wt, load_sem.at[5]))
    loads.append(pltpu.make_async_copy(w_out1, wto, load_sem.at[6]))
    for load in loads:
        load.start()

    barrier = pltpu.get_barrier_semaphore()
    greeted = [sibling, across] + [along(s) for s in (1, 2, 3)] + [peer(s) for s in range(1, 8)]
    for device in greeted:
        pl.semaphore_signal(barrier, inc=1, device_id=device, device_id_type=MESH)
    pl.semaphore_wait(barrier, len(greeted))

    def remote(src, dst, send, recv, device):
        return pltpu.make_async_remote_copy(
            src_ref=src, dst_ref=dst, send_sem=send, recv_sem=recv, device_id=device, device_id_type=MESH
        )

    def along_y(slot):
        step = STEPS[slot]
        return remote(tok.at[(y + 4 - step) % 4], x.at[0, slot, 0], y_send.at[slot], y_recv.at[slot], along(4 - step))

    def over_z(slot):
        return remote(x.at[0, slot, 0], x.at[1, slot, 0], z_send.at[slot], z_recv.at[slot], across)

    def to_sibling(half, slot):
        return remote(x.at[half, slot, 0], x.at[half, slot, 1], s_send.at[half, slot], s_recv.at[half, slot], sibling)

    def pass_on(slot):
        over_z(slot).start()
        to_sibling(0, slot).start()

    def pass_z(slot):
        over_z(slot).wait_recv()
        to_sibling(1, slot).start()

    table = [mod[part, 0:1, :] for part in range(3)]

    def project(half, slot):
        to_sibling(half, slot).wait_recv()
        mixed = modulate(x[half, slot].reshape(192, D), table)
        rows = pl.ds((half * 4 + slot) * 192, 192)
        if half == 0:
            queries = (nn_dot(mixed, w[:, :WIN]) * SCALE).astype(jnp.bfloat16)
            for quarter in range(2):
                for g in range(3):
                    q[pl.ds(g * 256 + quarter * 128 + slot * 32, 32), :] = queries[
                        quarter * 96 + g * 32 : quarter * 96 + g * 32 + 32
                    ]
        k[rows, :] = nn_dot(mixed, w[:, WIN : 2 * WIN]).astype(jnp.bfloat16)
        v[rows, :] = nn_dot(mixed, w[:, 2 * WIN :]).astype(jnp.bfloat16)

    along_y(1).start()
    along_y(2).start()
    loads[0].wait()
    pass_on(0)
    along_y(1).wait_send()
    along_y(3).start()
    for load in loads[1:4]:
        load.wait()
    project(0, 0)
    along_y(1).wait_recv()
    pass_on(1)
    along_y(2).wait_recv()
    pass_on(2)
    pass_z(0)
    project(0, 1)
    project(0, 2)
    along_y(3).wait_recv()
    pass_on(3)
    project(1, 0)
    project(0, 3)

    def starts(j):
        return ((16 * j + 64 * core, 255), (16 * j + 72 + 64 * core, 0))

    def early(g, carry):
        @pl.when(g > 0)
        def _():
            pass_z(g)

        rows = pl.ds(pl.multiple_of(g * 256, 256), 256)
        held = jnp.zeros((256, 128), jnp.float32)
        for j in range(4):
            window = slice(128 * j, 128 * j + 256)
            queries, keys, values = q[rows, window], k[:EARLY, window], v[:EARLY, window]
            both = jnp.zeros((256, 256), jnp.float32)
            for odd, (start, free) in enumerate(starts(j)):
                mine = head_lanes(start)
                scores = nt_dot(choose(queries, mine), keys)
                top = jnp.max(scores, axis=-1, keepdims=True)
                weights = jnp.exp2(scores - top).astype(jnp.bfloat16)
                part = nn_dot(weights, count_in(values, free))
                both = jnp.where(mine, part, both)
                held = jnp.where(lanes(128) == 2 * j + odd, top, held)
                held = jnp.where(lanes(128) == 8 + 2 * j + odd, part[:, free : free + 1], held)
            first[j, rows] = both
        stat[rows] = held
        return carry

    def late(g, j, carry):
        rows = pl.ds(pl.multiple_of(g * 256, 256), 256)
        window = slice(128 * j, 128 * j + 256)
        queries, keys, values = q[rows, window], k[EARLY:, window], v[EARLY:, window]
        held = stat[rows]
        both = jnp.zeros((256, 256), jnp.float32)
        factor = jnp.zeros((256, 256), jnp.float32)
        for odd, (start, free) in enumerate(starts(j)):
            mine = head_lanes(start)
            scores = nt_dot(choose(queries, mine), keys)
            before = held[:, 2 * j + odd : 2 * j + odd + 1]
            top = jnp.maximum(before, jnp.max(scores, axis=-1, keepdims=True))
            weights = jnp.exp2(scores - top).astype(jnp.bfloat16)
            part = nn_dot(weights, count_in(values, free))
            shrink = jnp.exp2(before - top)
            share = 1.0 / (held[:, 8 + 2 * j + odd : 9 + 2 * j + odd] * shrink + part[:, free : free + 1])
            both = jnp.where(mine, part * share, both)
            factor = jnp.where(mine, shrink * share, factor)
        both = both + first[j, rows] * factor
        att[g, :, 128 * j : 128 * j + 128] = (carry + both[:, :128]).astype(jnp.bfloat16)
        if j == 3:
            att[g, :, 512:] = both[:, 128:].astype(jnp.bfloat16)
        return both[:, 128:]

    def swap(g):
        return remote(att.at[g, pl.ds(128, 128)], att_in.at[g], a_send.at[g], a_recv.at[g], sibling)

    def give(g, slot):
        return remote(u.at[g, slot], gathered.at[g, y], u_send.at[g, slot], u_recv.at[g, slot], along(STEPS[slot]))

    def own_give(g):
        return pltpu.make_async_copy(u.at[g, 0], gathered.at[g, y], own_sem.at[0, g])

    def finish(g):
        swap(g).wait_recv()
        mine = pl.ds(pl.multiple_of(core * 512, 128), WIN)
        other = pl.ds(pl.multiple_of((1 - core) * 512, 128), WIN)
        flat = nn_dot(att[g, :128], wo[mine, :]) + nn_dot(att_in[g], wo[other, :])
        values = x[0, :, 0, pl.ds(pl.multiple_of(g * 32, 32), 32), :].astype(jnp.float32)
        u[g] = (values + table[2] * flat.reshape(4, 32, D)).astype(jnp.bfloat16)
        for slot in range(1, 4):
            give(g, slot).start()
        own_give(g).start()

    lax.fori_loop(0, 3, early, 0)
    project(1, 1)
    project(1, 2)
    pass_z(3)
    project(1, 3)
    loads[4].wait()

    def turn(g, carry):
        edge = jnp.zeros((256, 128), jnp.float32)
        edge = late(g, 0, edge)
        edge = late(g, 1, edge)

        @pl.when(g > 0)
        def _():
            finish(g - 1)

        edge = late(g, 2, edge)
        late(g, 3, edge)
        swap(g).start()
        return carry

    lax.fori_loop(0, 3, turn, 0)
    finish(2)

    def spread(g, step):
        return remote(
            grouped.at[g, (frame + step) % 8], t.at[g, frame], g_send.at[g, step], g_recv.at[g, step], peer(step)
        )

    def own_spread(g):
        return pltpu.make_async_copy(grouped.at[g, frame], t.at[g, frame], own_sem.at[1, g])

    def collect(g, step):
        return remote(r.at[g, (frame + step) % 8], back.at[g, frame], r_send.at[g, step], r_recv.at[g, step], peer(step))

    def own_collect(g):
        return pltpu.make_async_copy(r.at[g, frame], back.at[g, frame], own_sem.at[2, g])

    forward = shuffle(True)

    def relay(g, carry):
        own_give(g).wait()
        for slot in range(1, 4):
            give(g, slot).wait_recv()
        grouped[g] = nn_dot(forward, gathered[g].reshape(128, D)).astype(jnp.bfloat16).reshape(8, 16, D)
        for step in range(1, 8):
            spread(g, step).start()
        own_spread(g).start()
        return carry

    lax.fori_loop(0, 3, relay, 0)
    loads[5].wait()
    loads[6].wait()

    a = lax.broadcasted_iota(jnp.int32, (128, 128), 0)
    b = lax.broadcasted_iota(jnp.int32, (128, 128), 1)
    bias = jnp.where(a % 4 == b % 4, 0.0, -1e30)
    table1 = [mod[part, 1:2, :] for part in range(3)]

    def block(g, carry):
        own_spread(g).wait()
        for step in range(1, 8):
            spread(g, step).wait_recv()
        values = t[g].reshape(128, D)
        mixed = modulate(values, table1)
        packed[:, :D] = (nn_dot(mixed, wt[:, :D]) * SCALE).astype(jnp.bfloat16)
        packed[:, D : 2 * D] = nn_dot(mixed, wt[:, D : 2 * D]).astype(jnp.bfloat16)
        packed[:, 2 * D :] = nn_dot(mixed, wt[:, 2 * D :]).astype(jnp.bfloat16)
        spots = []
        scores = []
        for h in range(HEADS):
            at = 128 * min(HEAD * h // 128, 7)
            start = HEAD * h - at
            spots.append((at, head_lanes(start), 0 if start else 255))
            queries = choose(packed[:, at : at + 256], spots[h][1])
            scores.append(nt_dot(queries, packed[:, D + at : D + at + 256]) + bias)
        weights = []
        for h in range(HEADS):
            top = jnp.max(scores[h], axis=-1, keepdims=True)
            weights.append(jnp.exp2(scores[h] - top).astype(jnp.bfloat16))
        tiles = [None] * 9
        for h, (at, mine, free) in enumerate(spots):
            part = nn_dot(weights[h], count_in(packed[:, 2 * D + at : 2 * D + at + 256], free))
            part = jnp.where(mine, part * (1.0 / part[:, free : free + 1]), 0.0)
            for side in range(2):
                tile = at // 128 + side
                piece = part[:, 128 * side : 128 * side + 128]
                tiles[tile] = piece if tiles[tile] is None else tiles[tile] + piece
        for tile in range(9):
            mixed_t[:, 128 * tile : 128 * tile + 128] = tiles[tile].astype(jnp.bfloat16)
        flat = nn_dot(mixed_t[...], wto[...])
        r[g] = (values.astype(jnp.float32) + table1[2] * flat).astype(jnp.bfloat16).reshape(8, 16, D)
        for step in range(1, 8):
            collect(g, step).start()
        own_collect(g).start()
        return carry

    lax.fori_loop(0, 3, block, 0)

    backward = shuffle(False)

    def put(g):
        return pltpu.make_async_copy(res.at[g], out.at[:, pl.ds(pl.multiple_of(g * 32, 32), 32), :], o_sem.at[g])

    def settle(g, carry):
        own_collect(g).wait()
        for step in range(1, 8):
            collect(g, step).wait_recv()
        res[g] = nn_dot(backward, back[g].reshape(128, D)).astype(jnp.bfloat16).reshape(4, 32, D)
        put(g).start()
        return carry

    lax.fori_loop(0, 3, settle, 0)

    along_y(2).wait_send()
    along_y(3).wait_send()
    for slot in range(4):
        over_z(slot).wait_send()
        to_sibling(0, slot).wait_send()
        to_sibling(1, slot).wait_send()

    def drain(g, carry):
        swap(g).wait_send()
        for slot in range(1, 4):
            give(g, slot).wait_send()
        for step in range(1, 8):
            spread(g, step).wait_send()
            collect(g, step).wait_send()
        put(g).wait()
        return carry

    lax.fori_loop(0, 3, drain, 0)


def shards(tokens, modulation, spatial_input, spatial_output, temporal_input, temporal_output):
    dma = pltpu.SemaphoreType.DMA
    held = pl.BlockSpec(memory_space=pl.ANY)

    def bf16(*shape):
        return pltpu.VMEM(shape, jnp.bfloat16)

    return pl.pallas_call(
        kernel,
        out_shape=jax.ShapeDtypeStruct((4, 96, D), jnp.bfloat16),
        in_specs=[held, pl.BlockSpec(memory_space=pltpu.VMEM), held, held, held, held],
        out_specs=held,
        scratch_shapes=[
            bf16(2, 4, 2, 96, D),
            bf16(D, 3 * WIN),
            bf16(D, D),
            bf16(768, WIN),
            bf16(1536, WIN),
            bf16(1536, WIN),
            pltpu.VMEM((4, 768, 256), jnp.float32),
            pltpu.VMEM((768, 128), jnp.float32),
            bf16(3, 256, WIN),
            bf16(3, 128, WIN),
            bf16(3, 4, 32, D),
            bf16(3, 4, 32, D),
            bf16(D, 3 * D),
            bf16(D, D),
            bf16(3, 8, 16, D),
            bf16(3, 8, 16, D),
            bf16(128, 3 * D),
            bf16(128, D),
            bf16(3, 8, 16, D),
            bf16(3, 8, 16, D),
            bf16(3, 4, 32, D),
            dma((7,)),
            dma((4,)), dma((4,)),
            dma((2, 4)), dma((2, 4)),
            dma((4,)), dma((4,)),
            dma((3,)), dma((3,)),
            dma((3, 4)), dma((3, 4)),
            dma((3, 8)), dma((3, 8)),
            dma((3, 8)), dma((3, 8)),
            dma((3, 3)),
            dma((3,)),
        ],
        compiler_params=pltpu.CompilerParams(
            collective_id=0, has_side_effects=True, vmem_limit_bytes=VMEM_LIMIT
        ),
        name="block_pair",
    )(tokens, jnp.transpose(modulation, (1, 0, 2)), spatial_input, spatial_output, temporal_input, temporal_output)


def solution(mesh):
    in_specs = (P("frame", "patch", None), P(), P(), P(), P(), P())
    out_specs = P("frame", "patch", None)
    return jax.shard_map(shards, mesh=mesh, in_specs=in_specs, out_specs=out_specs, check_vma=False)
```

time: 505 us -> 85.1 us (0.17)
  waiting for transfers between devices: 171 us -> 0 us
  local copies, waits for them, and re-layouts: 108 us -> 2.15 us
  blocking collectives: 88.7 us -> 0 us
  Pallas kernels: 0 us -> 82.8 us
  matrix products: 64.6 us -> 0 us
  other arithmetic: 56.8 us -> 0 us
  between operations: 13.5 us -> 0.01 us
    all_gather x2 -> x0, waiting for transfers between devices: 171 us -> none  [the longest x1 129 us: shards(): lax.all_gather(packed[:, :, 1], 'patch', axis=1, tiled=True)]
    all_to_all x2 -> x0, blocking collectives: 88.7 us -> none  [the longest x1 63.3 us: shards(): lax.all_to_all(packed, 'frame', split_axis=1, concat_axis=0, tiled=True)]
    pallas_call x0 -> x1, Pallas kernels: none -> 82.8 us  [shards(): pl.pallas_call(kernel, out_shape=jax.ShapeDtypeStruct((4, 96, D), jnp.bfl...]
    dot_general x8 -> x0, matrix products: 64.6 us -> none  [the longest x1 19.7 us: attend_batch(): jnp.einsum('bhqk,bkhe->bqhe', weights, values, preferred_element_type=jnp...]
    all_gather x2 -> x0, local copies, waits for them, and re-layouts: 59.5 us -> none  [the longest x1 29.9 us: shards(): lax.all_gather(packed[:, :, 1], 'patch', axis=1, tiled=True)]
    sub x2 -> x0, other arithmetic: 50 us -> none  [softmax_rows(): expo = jnp.exp(scores - top)]
    reshape x3 -> x0, local copies, waits for them, and re-layouts: 22.1 us -> none  [project_in(): return flat.astype(jnp.bfloat16).reshape(lead + (3, HEADS, HEAD))]
    slice x3 -> x0, local copies, waits for them, and re-layouts: 13.6 us -> none  [the longest x2 9.15 us: shards(): packed[:, :, 2]]
  transfers between devices with their start and end apart: 2 -> 0, of which waited for: 2 -> 0; matrix products, arithmetic and copies ran while one was open for 19% -> 0% of each run, Pallas kernels for 0% -> 0%
where the time goes in v2:
time: 85.1 us; the launch traced here: 84.9 us
  Pallas kernels  82.8 us (97%)
  local copies, waits for them, and re-layouts  2.15 us (3%)
    pallas_call x1, Pallas kernels, shards(): pl.pallas_call(kernel, out_shape=jax.ShapeDtypeStruct((4, 96, D), jnp.bfl...  82.8 us
    unnamed x1, local copies, waits for them, and re-layouts  2.15 us

profile of v2, /device:TPU:0, one launch (start us, length us, event | category | flops | bytes accessed | tf_op | source)
XLA Modules:
  0.0 84.9 jit_solution(14912202842343530704)
XLA Ops:
  0.0 82.8 %block_pair.1 = bf16[4,96,1152]{2,1,0:T(8,128)(2,1)} custom-call(bf16[4,96,1152]{2,1,0:T(8,128)(2,1)} %tok.1, f32[3,2,1152]{2,1,0:T(2,128)} %bitcast.1, bf16[1152,3456]{1,0:T(8,128)(2,1)} %w_in0.1, bf16[1152,1152]{1,0:T(8,128)(2,1)} %w_out0.1, bf16[1152,3456]{1,0:T(8,128)(2,1)} %w_in1.1, bf16[1152,1152]{1,0:T(8,128)(2,1)} %w_out1.1), custom_call_target="tpu_custom_call" | custom-call | tf_op jit(solution)/shard_map/block_pair/pallas_call | solution.py:374
  82.8 2.1 %copy.8 = bf16[4,96,1152]{2,1,0:T(8,128)(2,1)} copy(bf16[4,96,1152]{2,1,0:T(8,128)(2,1)} %block_pair.1) | data formatting | bytes 1769472

commit v3 on v2

--- a/solution.py
+++ b/solution.py
@@ -11,7 +11,8 @@
 HEADS = 16
 HEAD = 72
 WIN = 640
-EARLY = 960
+EARLY = 1152
+LATE = 384
 SCALE = math.log2(math.e) / math.sqrt(HEAD)
 MESH = pl.DeviceIdType.MESH
 VMEM_LIMIT = 60 * 1024 * 1024
@@ -65,7 +66,7 @@
     x, w, wo, q, k, v, first, stat, att, att_in, u, gathered,
     wt, wto, grouped, t, packed, mixed_t, r, back, res,
     load_sem, y_send, y_recv, s_send, s_recv, z_send, z_recv, a_send, a_recv,
-    u_send, u_recv, g_send, g_recv, r_send, r_recv, own_sem, o_sem,
+    u_send, u_recv, g_send, g_recv, r_send, r_recv, own_sem, o_sem, meet_sem,
 ):
     frame = lax.axis_index("frame")
     patch = lax.axis_index("patch")
@@ -80,6 +81,12 @@
 
     def peer(step):
         return ((frame + step) % 8, patch)
+
+    def beside_x(step):
+        return ((frame // 4) * 4 + (frame + step) % 4, patch)
+
+    opposite = ((frame + 4) % 8, patch)
+    over_edge = ((frame + 4) % 8, y * 4 + (1 - z) * 2 + core)
 
     loads = [pltpu.make_async_copy(tok.at[y], x.at[0, 0, 0], load_sem.at[0])]
     for part in range(3):
@@ -90,14 +97,18 @@
     loads.append(pltpu.make_async_copy(w_out0, wo, load_sem.at[4]))
     loads.append(pltpu.make_async_copy(w_in1, wt, load_sem.at[5]))
     loads.append(pltpu.make_async_copy(w_out1, wto, load_sem.at[6]))
-    for load in loads:
+    for load in loads[:4]:
         load.start()
 
     barrier = pltpu.get_barrier_semaphore()
-    greeted = [sibling, across] + [along(s) for s in (1, 2, 3)] + [peer(s) for s in range(1, 8)]
+    beside = [beside_x(1), beside_x(3)]
+    greeted = [sibling, across] + [along(s) for s in (1, 2, 3)] + beside + [over_edge]
     for device in greeted:
         pl.semaphore_signal(barrier, inc=1, device_id=device, device_id_type=MESH)
     pl.semaphore_wait(barrier, len(greeted))
+
+    for device in beside + [across]:
+        pl.semaphore_signal(meet_sem.at[0], inc=1, device_id=device, device_id_type=MESH)
 
     def remote(src, dst, send, recv, device):
         return pltpu.make_async_remote_copy(
@@ -146,7 +157,11 @@
     along_y(3).start()
     for load in loads[1:4]:
         load.wait()
+    for load in loads[4:]:
+        load.start()
     project(0, 0)
+    pl.semaphore_wait(meet_sem.at[0], 3)
+    pl.semaphore_signal(meet_sem.at[1], inc=1, device_id=opposite, device_id_type=MESH)
     along_y(1).wait_recv()
     pass_on(1)
     along_y(2).wait_recv()
@@ -158,53 +173,52 @@
     pass_on(3)
     project(1, 0)
     project(0, 3)
+    pass_z(1)
+    project(1, 1)
 
     def starts(j):
         return ((16 * j + 64 * core, 255), (16 * j + 72 + 64 * core, 0))
 
     def early(g, carry):
-        @pl.when(g > 0)
+        @pl.when(g == 2)
         def _():
-            pass_z(g)
+            pass_z(2)
 
         rows = pl.ds(pl.multiple_of(g * 256, 256), 256)
-        held = jnp.zeros((256, 128), jnp.float32)
         for j in range(4):
             window = slice(128 * j, 128 * j + 256)
             queries, keys, values = q[rows, window], k[:EARLY, window], v[:EARLY, window]
-            both = jnp.zeros((256, 256), jnp.float32)
             for odd, (start, free) in enumerate(starts(j)):
-                mine = head_lanes(start)
-                scores = nt_dot(choose(queries, mine), keys)
+                scores = nt_dot(choose(queries, head_lanes(start)), keys)
                 top = jnp.max(scores, axis=-1, keepdims=True)
                 weights = jnp.exp2(scores - top).astype(jnp.bfloat16)
-                part = nn_dot(weights, count_in(values, free))
-                both = jnp.where(mine, part, both)
-                held = jnp.where(lanes(128) == 2 * j + odd, top, held)
-                held = jnp.where(lanes(128) == 8 + 2 * j + odd, part[:, free : free + 1], held)
-            first[j, rows] = both
-        stat[rows] = held
+                first[2 * j + odd, rows] = nn_dot(weights, count_in(values, free))
+                stat[2 * j + odd, rows] = jnp.broadcast_to(top, (256, 128))
         return carry
 
     def late(g, j, carry):
         rows = pl.ds(pl.multiple_of(g * 256, 256), 256)
         window = slice(128 * j, 128 * j + 256)
         queries, keys, values = q[rows, window], k[EARLY:, window], v[EARLY:, window]
-        held = stat[rows]
         both = jnp.zeros((256, 256), jnp.float32)
-        factor = jnp.zeros((256, 256), jnp.float32)
         for odd, (start, free) in enumerate(starts(j)):
+            h = 2 * j + odd
             mine = head_lanes(start)
             scores = nt_dot(choose(queries, mine), keys)
-            before = held[:, 2 * j + odd : 2 * j + odd + 1]
-            top = jnp.maximum(before, jnp.max(scores, axis=-1, keepdims=True))
-            weights = jnp.exp2(scores - top).astype(jnp.bfloat16)
+            parts = [scores[:, 128 * n : 128 * n + 128] for n in range(LATE // 128)]
+            top = parts[0]
+            for piece in parts[1:]:
+                top = jnp.maximum(top, piece)
+            before = stat[h, rows]
+            top = jnp.maximum(before, jnp.max(top, axis=-1, keepdims=True))
+            weights = jnp.concatenate([jnp.exp2(piece - top).astype(jnp.bfloat16) for piece in parts], axis=1)
             part = nn_dot(weights, count_in(values, free))
             shrink = jnp.exp2(before - top)
-            share = 1.0 / (held[:, 8 + 2 * j + odd : 9 + 2 * j + odd] * shrink + part[:, free : free + 1])
-            both = jnp.where(mine, part * share, both)
-            factor = jnp.where(mine, shrink * share, factor)
-        both = both + first[j, rows] * factor
+            earlier = first[h, rows]
+            total = jnp.concatenate(
+                [part[:, :128] + earlier[:, :128] * shrink, part[:, 128:] + earlier[:, 128:] * shrink], axis=1
+            )
+            both = jnp.where(mine, total * (1.0 / total[:, free : free + 1]), both)
         att[g, :, 128 * j : 128 * j + 128] = (carry + both[:, :128]).astype(jnp.bfloat16)
         if j == 3:
             att[g, :, 512:] = both[:, 128:].astype(jnp.bfloat16)
@@ -231,9 +245,8 @@
         own_give(g).start()
 
     lax.fori_loop(0, 3, early, 0)
-    project(1, 1)
+    pass_z(3)
     project(1, 2)
-    pass_z(3)
     project(1, 3)
     loads[4].wait()
 
@@ -269,6 +282,7 @@
         return pltpu.make_async_copy(r.at[g, frame], back.at[g, frame], own_sem.at[2, g])
 
     forward = shuffle(True)
+    pl.semaphore_wait(meet_sem.at[1], 1)
 
     def relay(g, carry):
         own_give(g).wait()
@@ -383,8 +397,8 @@
             bf16(768, WIN),
             bf16(1536, WIN),
             bf16(1536, WIN),
-            pltpu.VMEM((4, 768, 256), jnp.float32),
-            pltpu.VMEM((768, 128), jnp.float32),
+            pltpu.VMEM((8, 768, 256), jnp.float32),
+            pltpu.VMEM((8, 768, 128), jnp.float32),
             bf16(3, 256, WIN),
             bf16(3, 128, WIN),
             bf16(3, 4, 32, D),
@@ -408,6 +422,7 @@
             dma((3, 8)), dma((3, 8)),
             dma((3, 3)),
             dma((3,)),
+            pltpu.SemaphoreType.REGULAR((2,)),
         ],
         compiler_params=pltpu.CompilerParams(
             collective_id=0, has_side_effects=True, vmem_limit_bytes=VMEM_LIMIT

time: 85.1 us -> 76.2 us (0.90)
  Pallas kernels: 82.8 us -> 73.5 us
    pallas_call x1, Pallas kernels: 82.8 us -> 73.5 us  [shards(): pl.pallas_call(kernel, out_shape=jax.ShapeDtypeStruct((4, 96, D), jnp.bfl...]
where the time goes in v3:
time: 76.2 us; the launch traced here: 75.6 us
  Pallas kernels  73.5 us (96%)
  local copies, waits for them, and re-layouts  2.15 us (3%)
    pallas_call x1, Pallas kernels, shards(): pl.pallas_call(kernel, out_shape=jax.ShapeDtypeStruct((4, 96, D), jnp.bfl...  73.5 us
    unnamed x1, local copies, waits for them, and re-layouts  2.15 us

profile of v3, /device:TPU:0, one launch (start us, length us, event | category | flops | bytes accessed | tf_op | source)
XLA Modules:
  0.0 75.6 jit_solution(8158590173536773843)
XLA Ops:
  0.0 73.5 %block_pair.1 = bf16[4,96,1152]{2,1,0:T(8,128)(2,1)} custom-call(bf16[4,96,1152]{2,1,0:T(8,128)(2,1)} %tok.1, f32[3,2,1152]{2,1,0:T(2,128)} %bitcast.1, bf16[1152,3456]{1,0:T(8,128)(2,1)} %w_in0.1, bf16[1152,1152]{1,0:T(8,128)(2,1)} %w_out0.1, bf16[1152,3456]{1,0:T(8,128)(2,1)} %w_in1.1, bf16[1152,1152]{1,0:T(8,128)(2,1)} %w_out1.1), custom_call_target="tpu_custom_call" | custom-call | tf_op jit(solution)/shard_map/block_pair/pallas_call | solution.py:388
  73.5 2.1 %copy.8 = bf16[4,96,1152]{2,1,0:T(8,128)(2,1)} copy(bf16[4,96,1152]{2,1,0:T(8,128)(2,1)} %block_pair.1) | data formatting | bytes 1769472

commit v4 on v3

--- a/solution.py
+++ b/solution.py
@@ -63,7 +63,7 @@
 
 def kernel(
     tok, mod, w_in0, w_out0, w_in1, w_out1, out,
-    x, w, wo, q, k, v, first, stat, att, att_in, u, gathered,
+    x, m, w, wo, q, k, v, first, stat, att, att_in, u, gathered,
     wt, wto, grouped, t, packed, mixed_t, r, back, res,
     load_sem, y_send, y_recv, s_send, s_recv, z_send, z_recv, a_send, a_recv,
     u_send, u_recv, g_send, g_recv, r_send, r_recv, own_sem, o_sem, meet_sem,
@@ -88,7 +88,7 @@
     opposite = ((frame + 4) % 8, patch)
     over_edge = ((frame + 4) % 8, y * 4 + (1 - z) * 2 + core)
 
-    loads = [pltpu.make_async_copy(tok.at[y], x.at[0, 0, 0], load_sem.at[0])]
+    loads = [pltpu.make_async_copy(tok.at[y], x.at[0], load_sem.at[0])]
     for part in range(3):
         columns = pl.ds(pl.multiple_of(part * D + core * 512, 128), WIN)
         loads.append(
@@ -105,6 +105,9 @@
     greeted = [sibling, across] + [along(s) for s in (1, 2, 3)] + beside + [over_edge]
     for device in greeted:
         pl.semaphore_signal(barrier, inc=1, device_id=device, device_id_type=MESH)
+    table = [mod[part, 0:1, :] for part in range(3)]
+    loads[0].wait()
+    m[0, 0, 0] = modulate(x[0], table)
     pl.semaphore_wait(barrier, len(greeted))
 
     for device in beside + [across]:
@@ -117,15 +120,18 @@
 
     def along_y(slot):
         step = STEPS[slot]
-        return remote(tok.at[(y + 4 - step) % 4], x.at[0, slot, 0], y_send.at[slot], y_recv.at[slot], along(4 - step))
+        return remote(tok.at[(y + 4 - step) % 4], x.at[slot], y_send.at[slot], y_recv.at[slot], along(4 - step))
 
     def over_z(slot):
-        return remote(x.at[0, slot, 0], x.at[1, slot, 0], z_send.at[slot], z_recv.at[slot], across)
+        return remote(m.at[0, slot, 0], m.at[1, slot, 0], z_send.at[slot], z_recv.at[slot], across)
 
     def to_sibling(half, slot):
-        return remote(x.at[half, slot, 0], x.at[half, slot, 1], s_send.at[half, slot], s_recv.at[half, slot], sibling)
+        return remote(m.at[half, slot, 0], m.at[half, slot, 1], s_send.at[half, slot], s_recv.at[half, slot], sibling)
 
     def pass_on(slot):
+        if slot:
+            along_y(slot).wait_recv()
+            m[0, slot, 0] = modulate(x[slot], table)
         over_z(slot).start()
         to_sibling(0, slot).start()
 
@@ -133,25 +139,27 @@
         over_z(slot).wait_recv()
         to_sibling(1, slot).start()
 
-    table = [mod[part, 0:1, :] for part in range(3)]
-
-    def project(half, slot):
-        to_sibling(half, slot).wait_recv()
-        mixed = modulate(x[half, slot].reshape(192, D), table)
-        rows = pl.ds((half * 4 + slot) * 192, 192)
+    def project(half, slot, count):
+        for n in range(count):
+            to_sibling(half, slot + n).wait_recv()
+        mixed = m[half, slot : slot + count].reshape(192 * count, D)
+        rows = pl.ds((half * 4 + slot) * 192, 192 * count)
         if half == 0:
-            queries = (nn_dot(mixed, w[:, :WIN]) * SCALE).astype(jnp.bfloat16)
-            for quarter in range(2):
-                for g in range(3):
-                    q[pl.ds(g * 256 + quarter * 128 + slot * 32, 32), :] = queries[
-                        quarter * 96 + g * 32 : quarter * 96 + g * 32 + 32
-                    ]
-        k[rows, :] = nn_dot(mixed, w[:, WIN : 2 * WIN]).astype(jnp.bfloat16)
-        v[rows, :] = nn_dot(mixed, w[:, 2 * WIN :]).astype(jnp.bfloat16)
+            flat = nn_dot(mixed, w[...])
+            queries = (flat[:, :WIN] * SCALE).astype(jnp.bfloat16)
+            for n in range(count):
+                for quarter in range(2):
+                    for g in range(3):
+                        at = n * 192 + quarter * 96 + g * 32
+                        q[pl.ds(g * 256 + quarter * 128 + (slot + n) * 32, 32), :] = queries[at : at + 32]
+            flat = flat[:, WIN:]
+        else:
+            flat = nn_dot(mixed, w[:, WIN:])
+        k[rows, :] = flat[:, :WIN].astype(jnp.bfloat16)
+        v[rows, :] = flat[:, WIN:].astype(jnp.bfloat16)
 
     along_y(1).start()
     along_y(2).start()
-    loads[0].wait()
     pass_on(0)
     along_y(1).wait_send()
     along_y(3).start()
@@ -159,22 +167,17 @@
         load.wait()
     for load in loads[4:]:
         load.start()
-    project(0, 0)
+    project(0, 0, 1)
     pl.semaphore_wait(meet_sem.at[0], 3)
     pl.semaphore_signal(meet_sem.at[1], inc=1, device_id=opposite, device_id_type=MESH)
-    along_y(1).wait_recv()
     pass_on(1)
-    along_y(2).wait_recv()
     pass_on(2)
     pass_z(0)
-    project(0, 1)
-    project(0, 2)
-    along_y(3).wait_recv()
+    project(0, 1, 2)
     pass_on(3)
-    project(1, 0)
-    project(0, 3)
+    project(0, 3, 1)
     pass_z(1)
-    project(1, 1)
+    project(1, 0, 2)
 
     def starts(j):
         return ((16 * j + 64 * core, 255), (16 * j + 72 + 64 * core, 0))
@@ -238,7 +241,7 @@
         mine = pl.ds(pl.multiple_of(core * 512, 128), WIN)
         other = pl.ds(pl.multiple_of((1 - core) * 512, 128), WIN)
         flat = nn_dot(att[g, :128], wo[mine, :]) + nn_dot(att_in[g], wo[other, :])
-        values = x[0, :, 0, pl.ds(pl.multiple_of(g * 32, 32), 32), :].astype(jnp.float32)
+        values = x[:, pl.ds(pl.multiple_of(g * 32, 32), 32), :].astype(jnp.float32)
         u[g] = (values + table[2] * flat.reshape(4, 32, D)).astype(jnp.bfloat16)
         for slot in range(1, 4):
             give(g, slot).start()
@@ -246,8 +249,7 @@
 
     lax.fori_loop(0, 3, early, 0)
     pass_z(3)
-    project(1, 2)
-    project(1, 3)
+    project(1, 2, 2)
     loads[4].wait()
 
     def turn(g, carry):
@@ -391,6 +393,7 @@
         in_specs=[held, pl.BlockSpec(memory_space=pltpu.VMEM), held, held, held, held],
         out_specs=held,
         scratch_shapes=[
+            bf16(4, 96, D),
             bf16(2, 4, 2, 96, D),
             bf16(D, 3 * WIN),
             bf16(D, D),

time: 76.2 us -> 77.7 us (1.020)
  Pallas kernels: 73.5 us -> 75 us
    pallas_call x1, Pallas kernels: 73.5 us -> 75 us  [shards(): pl.pallas_call(kernel, out_shape=jax.ShapeDtypeStruct((4, 96, D), jnp.bfl...]
where the time goes in v4:
time: 77.7 us; the launch traced here: 77.2 us
  Pallas kernels  75 us (97%)
  local copies, waits for them, and re-layouts  2.15 us (3%)
    pallas_call x1, Pallas kernels, shards(): pl.pallas_call(kernel, out_shape=jax.ShapeDtypeStruct((4, 96, D), jnp.bfl...  75 us
    unnamed x1, local copies, waits for them, and re-layouts  2.15 us

profile of v4, /device:TPU:0, one launch (start us, length us, event | category | flops | bytes accessed | tf_op | source)
XLA Modules:
  0.0 77.2 jit_solution(13843124289697802154)
XLA Ops:
  0.0 75.0 %block_pair.1 = bf16[4,96,1152]{2,1,0:T(8,128)(2,1)} custom-call(bf16[4,96,1152]{2,1,0:T(8,128)(2,1)} %tok.1, f32[3,2,1152]{2,1,0:T(2,128)} %bitcast.1, bf16[1152,3456]{1,0:T(8,128)(2,1)} %w_in0.1, bf16[1152,1152]{1,0:T(8,128)(2,1)} %w_out0.1, bf16[1152,3456]{1,0:T(8,128)(2,1)} %w_in1.1, bf16[1152,1152]{1,0:T(8,128)(2,1)} %w_out1.1), custom_call_target="tpu_custom_call" | custom-call | tf_op jit(solution)/shard_map/block_pair/pallas_call | solution.py:390
  75.1 2.1 %copy.8 = bf16[4,96,1152]{2,1,0:T(8,128)(2,1)} copy(bf16[4,96,1152]{2,1,0:T(8,128)(2,1)} %block_pair.1) | data formatting | bytes 1769472

commit v5 on v4

--- a/solution.py
+++ b/solution.py
@@ -11,8 +11,9 @@
 HEADS = 16
 HEAD = 72
 WIN = 640
-EARLY = 1152
-LATE = 384
+EARLY = 768
+LATE = 768
+PLACES = ((0, 1, 2, 4), (3, 5, 6, 7))
 SCALE = math.log2(math.e) / math.sqrt(HEAD)
 MESH = pl.DeviceIdType.MESH
 VMEM_LIMIT = 60 * 1024 * 1024
@@ -62,8 +63,8 @@
 
 
 def kernel(
-    tok, mod, w_in0, w_out0, w_in1, w_out1, out,
-    x, m, w, wo, q, k, v, first, stat, att, att_in, u, gathered,
+    tok, mod_in, w_in0, w_out0, w_in1, w_out1, out,
+    mod, x, m, w, wo, q, k, v, first, stat, att, att_in, u, gathered,
     wt, wto, grouped, t, packed, mixed_t, r, back, res,
     load_sem, y_send, y_recv, s_send, s_recv, z_send, z_recv, a_send, a_recv,
     u_send, u_recv, g_send, g_recv, r_send, r_recv, own_sem, o_sem, meet_sem,
@@ -97,7 +98,8 @@
     loads.append(pltpu.make_async_copy(w_out0, wo, load_sem.at[4]))
     loads.append(pltpu.make_async_copy(w_in1, wt, load_sem.at[5]))
     loads.append(pltpu.make_async_copy(w_out1, wto, load_sem.at[6]))
-    for load in loads[:4]:
+    loads.append(pltpu.make_async_copy(mod_in, mod, load_sem.at[7]))
+    for load in [loads[7]] + loads[:4]:
         load.start()
 
     barrier = pltpu.get_barrier_semaphore()
@@ -105,6 +107,7 @@
     greeted = [sibling, across] + [along(s) for s in (1, 2, 3)] + beside + [over_edge]
     for device in greeted:
         pl.semaphore_signal(barrier, inc=1, device_id=device, device_id_type=MESH)
+    loads[7].wait()
     table = [mod[part, 0:1, :] for part in range(3)]
     loads[0].wait()
     m[0, 0, 0] = modulate(x[0], table)
@@ -118,91 +121,109 @@
             src_ref=src, dst_ref=dst, send_sem=send, recv_sem=recv, device_id=device, device_id_type=MESH
         )
 
-    def along_y(slot):
+    def rows_of(piece):
+        return pl.ds(piece * 48, 48)
+
+    def along_y(slot, piece):
         step = STEPS[slot]
-        return remote(tok.at[(y + 4 - step) % 4], x.at[slot], y_send.at[slot], y_recv.at[slot], along(4 - step))
-
-    def over_z(slot):
-        return remote(m.at[0, slot, 0], m.at[1, slot, 0], z_send.at[slot], z_recv.at[slot], across)
-
-    def to_sibling(half, slot):
-        return remote(m.at[half, slot, 0], m.at[half, slot, 1], s_send.at[half, slot], s_recv.at[half, slot], sibling)
-
-    def pass_on(slot):
-        if slot:
-            along_y(slot).wait_recv()
-            m[0, slot, 0] = modulate(x[slot], table)
-        over_z(slot).start()
-        to_sibling(0, slot).start()
+        rows = rows_of(piece)
+        return remote(
+            tok.at[(y + 4 - step) % 4, rows], x.at[slot, rows],
+            y_send.at[slot, piece], y_recv.at[slot, piece], along(4 - step),
+        )
+
+    def over_z(slot, piece):
+        rows = rows_of(piece)
+        return remote(
+            m.at[0, slot, 0, rows], m.at[1, slot, 0, rows], z_send.at[slot, piece], z_recv.at[slot, piece], across
+        )
+
+    def to_sibling(half, slot, piece):
+        rows = rows_of(piece)
+        return remote(
+            m.at[half, slot, 0, rows], m.at[half, slot, 1, rows],
+            s_send.at[half, slot, piece], s_recv.at[half, slot, piece], sibling,
+        )
+
+    def arrive(slot, piece):
+        along_y(slot, piece).wait_recv()
+        rows = rows_of(piece)
+        m[0, slot, 0, rows] = modulate(x[slot, rows], table)
+        over_z(slot, piece).start()
+        to_sibling(0, slot, piece).start()
 
     def pass_z(slot):
-        over_z(slot).wait_recv()
-        to_sibling(1, slot).start()
-
-    def project(half, slot, count):
+        for piece in range(2):
+            over_z(slot, piece).wait_recv()
+            to_sibling(1, slot, piece).start()
+
+    def project(half, slot, count, quarters=(0, 1)):
+        if 1 in quarters:
+            for n in range(count):
+                for piece in range(2):
+                    to_sibling(half, slot + n, piece).wait_recv()
+        chosen = slice(quarters[0], quarters[-1] + 1)
+        mixed = m[half, slot : slot + count, chosen].reshape(96 * len(quarters) * count, D)
+        flat = nn_dot(mixed, w[...] if half == 0 else w[:, WIN:])
+        if half == 0:
+            queries = (flat[:, :WIN] * SCALE).astype(jnp.bfloat16)
+            flat = flat[:, WIN:]
+        flat = flat.astype(jnp.bfloat16)
         for n in range(count):
-            to_sibling(half, slot + n).wait_recv()
-        mixed = m[half, slot : slot + count].reshape(192 * count, D)
-        rows = pl.ds((half * 4 + slot) * 192, 192 * count)
-        if half == 0:
-            flat = nn_dot(mixed, w[...])
-            queries = (flat[:, :WIN] * SCALE).astype(jnp.bfloat16)
-            for n in range(count):
-                for quarter in range(2):
-                    for g in range(3):
-                        at = n * 192 + quarter * 96 + g * 32
-                        q[pl.ds(g * 256 + quarter * 128 + (slot + n) * 32, 32), :] = queries[at : at + 32]
-            flat = flat[:, WIN:]
-        else:
-            flat = nn_dot(mixed, w[:, WIN:])
-        k[rows, :] = flat[:, :WIN].astype(jnp.bfloat16)
-        v[rows, :] = flat[:, WIN:].astype(jnp.bfloat16)
-
-    along_y(1).start()
-    along_y(2).start()
-    pass_on(0)
-    along_y(1).wait_send()
-    along_y(3).start()
+            for index, quarter in enumerate(quarters):
+                at = (n * len(quarters) + index) * 96
+                if half == 0:
+                    q[quarter, slot + n] = queries[at : at + 96].reshape(3, 32, WIN)
+                rows = pl.ds(PLACES[half][slot + n] * 192 + quarter * 96, 96)
+                k[rows, :] = flat[at : at + 96, :WIN]
+                v[rows, :] = flat[at : at + 96, WIN:]
+
+    for piece in range(2):
+        along_y(1, piece).start()
+        along_y(2, piece).start()
+    for piece in range(2):
+        over_z(0, piece).start()
+        to_sibling(0, 0, piece).start()
     for load in loads[1:4]:
         load.wait()
-    for load in loads[4:]:
+    for load in loads[4:7]:
         load.start()
     project(0, 0, 1)
+    arrive(1, 0)
+    arrive(2, 0)
+    for piece in range(2):
+        along_y(1, piece).wait_send()
+        along_y(3, piece).start()
+    arrive(1, 1)
+    arrive(2, 1)
+    project(0, 1, 2, (0,))
+    pass_z(0)
+    project(0, 1, 2, (1,))
+    project(1, 0, 1)
     pl.semaphore_wait(meet_sem.at[0], 3)
     pl.semaphore_signal(meet_sem.at[1], inc=1, device_id=opposite, device_id_type=MESH)
-    pass_on(1)
-    pass_on(2)
-    pass_z(0)
-    project(0, 1, 2)
-    pass_on(3)
-    project(0, 3, 1)
-    pass_z(1)
-    project(1, 0, 2)
 
     def starts(j):
         return ((16 * j + 64 * core, 255), (16 * j + 72 + 64 * core, 0))
 
-    def early(g, carry):
-        @pl.when(g == 2)
-        def _():
-            pass_z(2)
-
-        rows = pl.ds(pl.multiple_of(g * 256, 256), 256)
+    def early(part, count):
         for j in range(4):
             window = slice(128 * j, 128 * j + 256)
-            queries, keys, values = q[rows, window], k[:EARLY, window], v[:EARLY, window]
+            queries = q[part + (slice(None), slice(None), window)]
+            shape = queries.shape[:3]
+            queries, keys, values = queries.reshape(count, 256), k[:EARLY, window], v[:EARLY, window]
             for odd, (start, free) in enumerate(starts(j)):
                 scores = nt_dot(choose(queries, head_lanes(start)), keys)
                 top = jnp.max(scores, axis=-1, keepdims=True)
                 weights = jnp.exp2(scores - top).astype(jnp.bfloat16)
-                first[2 * j + odd, rows] = nn_dot(weights, count_in(values, free))
-                stat[2 * j + odd, rows] = jnp.broadcast_to(top, (256, 128))
-        return carry
+                total = nn_dot(weights, count_in(values, free))
+                first[(2 * j + odd,) + part] = total.reshape(shape + (256,))
+                stat[(2 * j + odd,) + part] = jnp.broadcast_to(top, (count, 128)).reshape(shape + (128,))
 
     def late(g, j, carry):
-        rows = pl.ds(pl.multiple_of(g * 256, 256), 256)
         window = slice(128 * j, 128 * j + 256)
-        queries, keys, values = q[rows, window], k[EARLY:, window], v[EARLY:, window]
+        queries = q[:, :, g, :, window].reshape(256, 256)
+        keys, values = k[EARLY:, window], v[EARLY:, window]
         both = jnp.zeros((256, 256), jnp.float32)
         for odd, (start, free) in enumerate(starts(j)):
             h = 2 * j + odd
@@ -212,12 +233,12 @@
             top = parts[0]
             for piece in parts[1:]:
                 top = jnp.maximum(top, piece)
-            before = stat[h, rows]
+            before = stat[h, :, :, g].reshape(256, 128)
             top = jnp.maximum(before, jnp.max(top, axis=-1, keepdims=True))
             weights = jnp.concatenate([jnp.exp2(piece - top).astype(jnp.bfloat16) for piece in parts], axis=1)
             part = nn_dot(weights, count_in(values, free))
             shrink = jnp.exp2(before - top)
-            earlier = first[h, rows]
+            earlier = first[h, :, :, g].reshape(256, 256)
             total = jnp.concatenate(
                 [part[:, :128] + earlier[:, :128] * shrink, part[:, 128:] + earlier[:, 128:] * shrink], axis=1
             )
@@ -247,9 +268,17 @@
             give(g, slot).start()
         own_give(g).start()
 
-    lax.fori_loop(0, 3, early, 0)
+    early((0, slice(0, 3)), 288)
+    arrive(3, 0)
+    arrive(3, 1)
+    early((1, slice(0, 3)), 288)
+    project(0, 3, 1)
+    pass_z(1)
+    pass_z(2)
+    early((slice(0, 2), 3), 192)
+    project(1, 1, 2)
     pass_z(3)
-    project(1, 2, 2)
+    project(1, 3, 1)
     loads[4].wait()
 
     def turn(g, carry):
@@ -360,12 +389,13 @@
 
     lax.fori_loop(0, 3, settle, 0)
 
-    along_y(2).wait_send()
-    along_y(3).wait_send()
-    for slot in range(4):
-        over_z(slot).wait_send()
-        to_sibling(0, slot).wait_send()
-        to_sibling(1, slot).wait_send()
+    for piece in range(2):
+        along_y(2, piece).wait_send()
+        along_y(3, piece).wait_send()
+        for slot in range(4):
+            over_z(slot, piece).wait_send()
+            to_sibling(0, slot, piece).wait_send()
+            to_sibling(1, slot, piece).wait_send()
 
     def drain(g, carry):
         swap(g).wait_send()
@@ -390,18 +420,19 @@
     return pl.pallas_call(
         kernel,
         out_shape=jax.ShapeDtypeStruct((4, 96, D), jnp.bfloat16),
-        in_specs=[held, pl.BlockSpec(memory_space=pltpu.VMEM), held, held, held, held],
+        in_specs=[held] * 6,
         out_specs=held,
         scratch_shapes=[
+            pltpu.VMEM((3, 2, D), jnp.float32),
             bf16(4, 96, D),
             bf16(2, 4, 2, 96, D),
             bf16(D, 3 * WIN),
             bf16(D, D),
-            bf16(768, WIN),
+            bf16(2, 4, 3, 32, WIN),
             bf16(1536, WIN),
             bf16(1536, WIN),
-            pltpu.VMEM((8, 768, 256), jnp.float32),
-            pltpu.VMEM((8, 768, 128), jnp.float32),
+            pltpu.VMEM((8, 2, 4, 3, 32, 256), jnp.float32),
+            pltpu.VMEM((8, 2, 4, 3, 32, 128), jnp.float32),
             bf16(3, 256, WIN),
             bf16(3, 128, WIN),
             bf16(3, 4, 32, D),
@@ -415,10 +446,10 @@
             bf16(3, 8, 16, D),
             bf16(3, 8, 16, D),
             bf16(3, 4, 32, D),
-            dma((7,)),
-            dma((4,)), dma((4,)),
-            dma((2, 4)), dma((2, 4)),
-            dma((4,)), dma((4,)),
+            dma((8,)),
+            dma((4, 2)), dma((4, 2)),
+            dma((2, 4, 2)), dma((2, 4, 2)),
+            dma((4, 2)), dma((4, 2)),
             dma((3,)), dma((3,)),
             dma((3, 4)), dma((3, 4)),
             dma((3, 8)), dma((3, 8)),

time: 77.7 us -> 72.3 us (0.931)
  Pallas kernels: 75 us -> 70 us
    pallas_call x1, Pallas kernels: 75 us -> 70 us  [shards(): pl.pallas_call(kernel, out_shape=jax.ShapeDtypeStruct((4, 96, D), jnp.bfl...]
where the time goes in v5:
time: 72.3 us; the launch traced here: 72.2 us
  Pallas kernels  70 us (97%)
  local copies, waits for them, and re-layouts  2.15 us (3%)
    pallas_call x1, Pallas kernels, shards(): pl.pallas_call(kernel, out_shape=jax.ShapeDtypeStruct((4, 96, D), jnp.bfl...  70 us
    unnamed x1, local copies, waits for them, and re-layouts  2.15 us

profile of v5, /device:TPU:0, one launch (start us, length us, event | category | flops | bytes accessed | tf_op | source)
XLA Modules:
  0.0 72.2 jit_solution(14347053881144929795)
XLA Ops:
  0.0 70.0 %block_pair.1 = bf16[4,96,1152]{2,1,0:T(8,128)(2,1)} custom-call(bf16[4,96,1152]{2,1,0:T(8,128)(2,1)} %tok.1, f32[3,2,1152]{2,1,0:T(2,128)} %bitcast.1, bf16[1152,3456]{1,0:T(8,128)(2,1)} %w_in0.1, bf16[1152,1152]{1,0:T(8,128)(2,1)} %w_out0.1, bf16[1152,3456]{1,0:T(8,128)(2,1)} %w_in1.1, bf16[1152,1152]{1,0:T(8,128)(2,1)} %w_out1.1), custom_call_target="tpu_custom_call" | custom-call | tf_op jit(solution)/shard_map/block_pair/pallas_call | solution.py:420
  70.0 2.1 %copy.8 = bf16[4,96,1152]{2,1,0:T(8,128)(2,1)} copy(bf16[4,96,1152]{2,1,0:T(8,128)(2,1)} %block_pair.1) | data formatting | bytes 1769472

commit v6 on v5

--- a/solution.py
+++ b/solution.py
@@ -206,19 +206,29 @@
     def starts(j):
         return ((16 * j + 64 * core, 255), (16 * j + 72 + 64 * core, 0))
 
-    def early(part, count):
+    def early(parts):
         for j in range(4):
             window = slice(128 * j, 128 * j + 256)
-            queries = q[part + (slice(None), slice(None), window)]
-            shape = queries.shape[:3]
-            queries, keys, values = queries.reshape(count, 256), k[:EARLY, window], v[:EARLY, window]
+            pieces = [q[part + (Ellipsis, window)] for part in parts]
+            shapes = [piece.shape[:-1] for piece in pieces]
+            counts = [math.prod(shape) for shape in shapes]
+            pieces = [piece.reshape(count, 256) for piece, count in zip(pieces, counts)]
+            queries = pieces[0] if len(pieces) == 1 else jnp.concatenate(pieces, axis=0)
+            keys, values = k[:EARLY, window], v[:EARLY, window]
             for odd, (start, free) in enumerate(starts(j)):
                 scores = nt_dot(choose(queries, head_lanes(start)), keys)
                 top = jnp.max(scores, axis=-1, keepdims=True)
                 weights = jnp.exp2(scores - top).astype(jnp.bfloat16)
                 total = nn_dot(weights, count_in(values, free))
-                first[(2 * j + odd,) + part] = total.reshape(shape + (256,))
-                stat[(2 * j + odd,) + part] = jnp.broadcast_to(top, (count, 128)).reshape(shape + (128,))
+                top = jnp.broadcast_to(top, (sum(counts), 128))
+                at = 0
+                for part, shape, count in zip(parts, shapes, counts):
+                    first[(2 * j + odd,) + part] = total[at : at + count].reshape(shape + (256,))
+                    stat[(2 * j + odd,) + part] = top[at : at + count].reshape(shape + (128,))
+                    at += count
+
+    def early_rest(g):
+        early([(1, slice(0, 3), g), (slice(0, 2), 3, g)])
 
     def late(g, j, carry):
         window = slice(128 * j, 128 * j + 256)
@@ -268,36 +278,6 @@
             give(g, slot).start()
         own_give(g).start()
 
-    early((0, slice(0, 3)), 288)
-    arrive(3, 0)
-    arrive(3, 1)
-    early((1, slice(0, 3)), 288)
-    project(0, 3, 1)
-    pass_z(1)
-    pass_z(2)
-    early((slice(0, 2), 3), 192)
-    project(1, 1, 2)
-    pass_z(3)
-    project(1, 3, 1)
-    loads[4].wait()
-
-    def turn(g, carry):
-        edge = jnp.zeros((256, 128), jnp.float32)
-        edge = late(g, 0, edge)
-        edge = late(g, 1, edge)
-
-        @pl.when(g > 0)
-        def _():
-            finish(g - 1)
-
-        edge = late(g, 2, edge)
-        late(g, 3, edge)
-        swap(g).start()
-        return carry
-
-    lax.fori_loop(0, 3, turn, 0)
-    finish(2)
-
     def spread(g, step):
         return remote(
             grouped.at[g, (frame + step) % 8], t.at[g, frame], g_send.at[g, step], g_recv.at[g, step], peer(step)
@@ -312,10 +292,7 @@
     def own_collect(g):
         return pltpu.make_async_copy(r.at[g, frame], back.at[g, frame], own_sem.at[2, g])
 
-    forward = shuffle(True)
-    pl.semaphore_wait(meet_sem.at[1], 1)
-
-    def relay(g, carry):
+    def relay(g):
         own_give(g).wait()
         for slot in range(1, 4):
             give(g, slot).wait_recv()
@@ -323,9 +300,44 @@
         for step in range(1, 8):
             spread(g, step).start()
         own_spread(g).start()
-        return carry
-
-    lax.fori_loop(0, 3, relay, 0)
+
+    early([(0, slice(0, 3))])
+    arrive(3, 0)
+    arrive(3, 1)
+    project(0, 3, 1)
+    early_rest(0)
+    pass_z(1)
+    pass_z(2)
+    early_rest(1)
+    project(1, 1, 2)
+    pass_z(3)
+    project(1, 3, 1)
+    loads[4].wait()
+
+    edge = jnp.zeros((256, 128), jnp.float32)
+
+    def late_pairs(g, pairs, edge):
+        for j in pairs:
+            edge = late(g, j, edge)
+        return edge
+
+    late_pairs(0, range(4), edge)
+    swap(0).start()
+    early_rest(2)
+    finish(0)
+    late_pairs(1, range(4), edge)
+    swap(1).start()
+    half = late_pairs(2, range(2), edge)
+    finish(1)
+    late_pairs(2, range(2, 4), half)
+    swap(2).start()
+    pl.semaphore_wait(meet_sem.at[1], 1)
+    forward = shuffle(True)
+    relay(0)
+    finish(2)
+    relay(1)
+    relay(2)
+
     loads[5].wait()
     loads[6].wait()
 

time: 72.3 us -> 75.7 us (1.047)
  Pallas kernels: 70 us -> 73.4 us
    pallas_call x1, Pallas kernels: 70 us -> 73.4 us  [shards(): pl.pallas_call(kernel, out_shape=jax.ShapeDtypeStruct((4, 96, D), jnp.bfl...]
where the time goes in v6:
time: 75.7 us; the launch traced here: 75.5 us
  Pallas kernels  73.4 us (97%)
  local copies, waits for them, and re-layouts  2.15 us (3%)
    pallas_call x1, Pallas kernels, shards(): pl.pallas_call(kernel, out_shape=jax.ShapeDtypeStruct((4, 96, D), jnp.bfl...  73.4 us
    unnamed x1, local copies, waits for them, and re-layouts  2.15 us

profile of v6, /device:TPU:0, one launch (start us, length us, event | category | flops | bytes accessed | tf_op | source)
XLA Modules:
  0.0 75.5 jit_solution(2298242540029920829)
XLA Ops:
  0.0 73.4 %block_pair.1 = bf16[4,96,1152]{2,1,0:T(8,128)(2,1)} custom-call(bf16[4,96,1152]{2,1,0:T(8,128)(2,1)} %tok.1, f32[3,2,1152]{2,1,0:T(2,128)} %bitcast.1, bf16[1152,3456]{1,0:T(8,128)(2,1)} %w_in0.1, bf16[1152,1152]{1,0:T(8,128)(2,1)} %w_out0.1, bf16[1152,3456]{1,0:T(8,128)(2,1)} %w_in1.1, bf16[1152,1152]{1,0:T(8,128)(2,1)} %w_out1.1), custom_call_target="tpu_custom_call" | custom-call | tf_op jit(solution)/shard_map/block_pair/pallas_call | solution.py:432
  73.4 2.1 %copy.8 = bf16[4,96,1152]{2,1,0:T(8,128)(2,1)} copy(bf16[4,96,1152]{2,1,0:T(8,128)(2,1)} %block_pair.1) | data formatting | bytes 1769472

commit v7 on v5

--- a/solution.py
+++ b/solution.py
@@ -17,6 +17,7 @@
 SCALE = math.log2(math.e) / math.sqrt(HEAD)
 MESH = pl.DeviceIdType.MESH
 VMEM_LIMIT = 60 * 1024 * 1024
+FAR_FIRST = (6, 5, 2, 7, 1, 4, 3)
 STEPS = (0, 1, 3, 2)
 
 
@@ -65,9 +66,9 @@
 def kernel(
     tok, mod_in, w_in0, w_out0, w_in1, w_out1, out,
     mod, x, m, w, wo, q, k, v, first, stat, att, att_in, u, gathered,
-    wt, wto, grouped, t, packed, mixed_t, r, back, res,
+    wt, wto, grouped, t, packed, mixed_t, r,
     load_sem, y_send, y_recv, s_send, s_recv, z_send, z_recv, a_send, a_recv,
-    u_send, u_recv, g_send, g_recv, r_send, r_recv, own_sem, o_sem, meet_sem,
+    u_send, u_recv, g_send, g_recv, r_send, r_recv, own_sem, meet_sem,
 ):
     frame = lax.axis_index("frame")
     patch = lax.axis_index("patch")
@@ -80,8 +81,11 @@
     def along(step):
         return (frame, ((y + step) % 4) * 4 + z * 2 + core)
 
+    def peer_frame(step):
+        return ((frame // 4 + step // 4) % 2) * 4 + (frame + step % 4) % 4
+
     def peer(step):
-        return ((frame + step) % 8, patch)
+        return (peer_frame(step), patch)
 
     def beside_x(step):
         return ((frame // 4) * 4 + (frame + step) % 4, patch)
@@ -296,21 +300,20 @@
         return carry
 
     lax.fori_loop(0, 3, turn, 0)
-    finish(2)
 
     def spread(g, step):
         return remote(
-            grouped.at[g, (frame + step) % 8], t.at[g, frame], g_send.at[g, step], g_recv.at[g, step], peer(step)
+            grouped.at[g, peer_frame(step)], t.at[g, frame], g_send.at[g, step], g_recv.at[g, step], peer(step)
         )
 
     def own_spread(g):
         return pltpu.make_async_copy(grouped.at[g, frame], t.at[g, frame], own_sem.at[1, g])
 
     def collect(g, step):
-        return remote(r.at[g, (frame + step) % 8], back.at[g, frame], r_send.at[g, step], r_recv.at[g, step], peer(step))
+        return remote(r.at[g, peer_frame(step)], out.at[g, frame], r_send.at[g, step], r_recv.at[g, step], peer(step))
 
     def own_collect(g):
-        return pltpu.make_async_copy(r.at[g, frame], back.at[g, frame], own_sem.at[2, g])
+        return pltpu.make_async_copy(r.at[g, frame], out.at[g, frame], own_sem.at[2, g])
 
     forward = shuffle(True)
     pl.semaphore_wait(meet_sem.at[1], 1)
@@ -320,12 +323,14 @@
         for slot in range(1, 4):
             give(g, slot).wait_recv()
         grouped[g] = nn_dot(forward, gathered[g].reshape(128, D)).astype(jnp.bfloat16).reshape(8, 16, D)
-        for step in range(1, 8):
+        for step in FAR_FIRST:
             spread(g, step).start()
         own_spread(g).start()
         return carry
 
-    lax.fori_loop(0, 3, relay, 0)
+    relay(0, 0)
+    finish(2)
+    lax.fori_loop(1, 3, relay, 0)
     loads[5].wait()
     loads[6].wait()
 
@@ -367,24 +372,17 @@
             mixed_t[:, 128 * tile : 128 * tile + 128] = tiles[tile].astype(jnp.bfloat16)
         flat = nn_dot(mixed_t[...], wto[...])
         r[g] = (values.astype(jnp.float32) + table1[2] * flat).astype(jnp.bfloat16).reshape(8, 16, D)
-        for step in range(1, 8):
+        for step in FAR_FIRST:
             collect(g, step).start()
         own_collect(g).start()
         return carry
 
     lax.fori_loop(0, 3, block, 0)
-
-    backward = shuffle(False)
-
-    def put(g):
-        return pltpu.make_async_copy(res.at[g], out.at[:, pl.ds(pl.multiple_of(g * 32, 32), 32), :], o_sem.at[g])
 
     def settle(g, carry):
         own_collect(g).wait()
         for step in range(1, 8):
             collect(g, step).wait_recv()
-        res[g] = nn_dot(backward, back[g].reshape(128, D)).astype(jnp.bfloat16).reshape(4, 32, D)
-        put(g).start()
         return carry
 
     lax.fori_loop(0, 3, settle, 0)
@@ -404,10 +402,16 @@
         for step in range(1, 8):
             spread(g, step).wait_send()
             collect(g, step).wait_send()
-        put(g).wait()
         return carry
 
     lax.fori_loop(0, 3, drain, 0)
+
+
+def reorder(back, out):
+    backward = shuffle(False)
+    for g in range(3):
+        rows = nn_dot(backward, back[g].reshape(128, D)).astype(jnp.bfloat16)
+        out[:, g * 32 : g * 32 + 32, :] = rows.reshape(4, 32, D)
 
 
 def shards(tokens, modulation, spatial_input, spatial_output, temporal_input, temporal_output):
@@ -417,9 +421,9 @@
     def bf16(*shape):
         return pltpu.VMEM(shape, jnp.bfloat16)
 
-    return pl.pallas_call(
+    back = pl.pallas_call(
         kernel,
-        out_shape=jax.ShapeDtypeStruct((4, 96, D), jnp.bfloat16),
+        out_shape=jax.ShapeDtypeStruct((3, 8, 16, D), jnp.bfloat16),
         in_specs=[held] * 6,
         out_specs=held,
         scratch_shapes=[
@@ -444,8 +448,6 @@
             bf16(128, 3 * D),
             bf16(128, D),
             bf16(3, 8, 16, D),
-            bf16(3, 8, 16, D),
-            bf16(3, 4, 32, D),
             dma((8,)),
             dma((4, 2)), dma((4, 2)),
             dma((2, 4, 2)), dma((2, 4, 2)),
@@ -455,7 +457,6 @@
             dma((3, 8)), dma((3, 8)),
             dma((3, 8)), dma((3, 8)),
             dma((3, 3)),
-            dma((3,)),
             pltpu.SemaphoreType.REGULAR((2,)),
         ],
         compiler_params=pltpu.CompilerParams(
@@ -463,6 +464,15 @@
         ),
         name="block_pair",
     )(tokens, jnp.transpose(modulation, (1, 0, 2)), spatial_input, spatial_output, temporal_input, temporal_output)
+    vmem = pl.BlockSpec(memory_space=pltpu.VMEM)
+    return pl.pallas_call(
+        reorder,
+        out_shape=jax.ShapeDtypeStruct((4, 96, D), jnp.bfloat16),
+        in_specs=[vmem],
+        out_specs=vmem,
+        compiler_params=pltpu.CompilerParams(vmem_limit_bytes=VMEM_LIMIT),
+        name="reorder",
+    )(back)
 
 
 def solution(mesh):

time: 72.3 us -> 71.6 us (level)
  local copies, waits for them, and re-layouts: 2.15 us -> 0 us
  Pallas kernels: 70 us -> 71.2 us
    unnamed x1 -> x0, local copies, waits for them, and re-layouts: 2.15 us -> none
    pallas_call x1 -> x2, Pallas kernels: 70 us -> 71.2 us  [the longest x1 68.7 us: shards(): pl.pallas_call(kernel, out_shape=jax.ShapeDtypeStruct((3, 8, 16, D), jnp....]
where the time goes in v7:
time: 71.6 us; the launch traced here: 71.2 us
  Pallas kernels  71.2 us (99%)
    pallas_call x1, Pallas kernels, shards(): pl.pallas_call(kernel, out_shape=jax.ShapeDtypeStruct((3, 8, 16, D), jnp....  68.7 us
    pallas_call x1, Pallas kernels, shards(): pl.pallas_call(reorder, out_shape=jax.ShapeDtypeStruct((4, 96, D), jnp.bf...  2.46 us

profile of v7, /device:TPU:0, one launch (start us, length us, event | category | flops | bytes accessed | tf_op | source)
XLA Modules:
  0.0 71.2 jit_solution(4258590298352690018)
XLA Ops:
  0.0 68.7 %block_pair.1.back = bf16[3,8,16,1152]{3,2,1,0:T(8,128)(2,1)} custom-call(bf16[4,96,1152]{2,1,0:T(8,128)(2,1)} %tok.1, f32[3,2,1152]{2,1,0:T(2,128)} %bitcast.1, bf16[1152,3456]{1,0:T(8,128)(2,1)} %w_in0.1, bf16[1152,1152]{1,0:T(8,128)(2,1)} %w_out0.1, bf16[1152,3456]{1,0:T(8,128)(2,1)} %w_in1.1, bf16[1152,1152]{1,0:T(8,128)(2,1)} %w_out1.1), custom_call_target="tpu_custom_call" | custom-call | tf_op jit(solution)/shard_map/block_pair/pallas_call | solution.py:424
  68.7 2.5 %reorder.1 = bf16[4,96,1152]{2,1,0:T(8,128)(2,1)} custom-call(bf16[3,8,16,1152]{3,2,1,0:T(8,128)(2,1)} %block_pair.1.back), custom_call_target="tpu_custom_call" | custom-call | tf_op jit(solution)/shard_map/reorder/pallas_call | solution.py:468

commit v8 on v7

--- a/solution.py
+++ b/solution.py
@@ -196,7 +196,6 @@
     arrive(1, 0)
     arrive(2, 0)
     for piece in range(2):
-        along_y(1, piece).wait_send()
         along_y(3, piece).start()
     arrive(1, 1)
     arrive(2, 1)
@@ -272,9 +271,9 @@
             give(g, slot).start()
         own_give(g).start()
 
-    early((0, slice(0, 3)), 288)
     arrive(3, 0)
     arrive(3, 1)
+    early((0, slice(0, 3)), 288)
     early((1, slice(0, 3)), 288)
     project(0, 3, 1)
     pass_z(1)
@@ -388,6 +387,7 @@
     lax.fori_loop(0, 3, settle, 0)
 
     for piece in range(2):
+        along_y(1, piece).wait_send()
         along_y(2, piece).wait_send()
         along_y(3, piece).wait_send()
         for slot in range(4):
@@ -408,10 +408,8 @@
 
 
 def reorder(back, out):
-    backward = shuffle(False)
-    for g in range(3):
-        rows = nn_dot(backward, back[g].reshape(128, D)).astype(jnp.bfloat16)
-        out[:, g * 32 : g * 32 + 32, :] = rows.reshape(4, 32, D)
+    rows = nn_dot(shuffle(False), back[0].reshape(128, D)).astype(jnp.bfloat16)
+    out[...] = rows.reshape(4, 32, D)
 
 
 def shards(tokens, modulation, spatial_input, spatial_output, temporal_input, temporal_output):
@@ -464,12 +462,12 @@
         ),
         name="block_pair",
     )(tokens, jnp.transpose(modulation, (1, 0, 2)), spatial_input, spatial_output, temporal_input, temporal_output)
-    vmem = pl.BlockSpec(memory_space=pltpu.VMEM)
     return pl.pallas_call(
         reorder,
         out_shape=jax.ShapeDtypeStruct((4, 96, D), jnp.bfloat16),
-        in_specs=[vmem],
-        out_specs=vmem,
+        grid=(3,),
+        in_specs=[pl.BlockSpec((1, 8, 16, D), lambda g: (g, 0, 0, 0))],
+        out_specs=pl.BlockSpec((4, 32, D), lambda g: (0, g, 0)),
         compiler_params=pltpu.CompilerParams(vmem_limit_bytes=VMEM_LIMIT),
         name="reorder",
     )(back)

time: 71.6 us -> 71.7 us (level)
    pallas_call x1, Pallas kernels: 2.46 us -> 3.21 us  [shards(): pl.pallas_call(reorder, out_shape=jax.ShapeDtypeStruct((4, 96, D), jnp.bf...]
where the time goes in v8:
time: 71.7 us; the launch traced here: 71.6 us
  Pallas kernels  71.6 us (100%)
    pallas_call x1, Pallas kernels, shards(): pl.pallas_call(kernel, out_shape=jax.ShapeDtypeStruct((3, 8, 16, D), jnp....  68.4 us
    pallas_call x1, Pallas kernels, shards(): pl.pallas_call(reorder, out_shape=jax.ShapeDtypeStruct((4, 96, D), jnp.bf...  3.21 us

profile of v8, /device:TPU:0, one launch (start us, length us, event | category | flops | bytes accessed | tf_op | source)
XLA Modules:
  0.0 71.6 jit_solution(5514851384372090139)
XLA Ops:
  0.0 68.4 %block_pair.1.back = bf16[3,8,16,1152]{3,2,1,0:T(8,128)(2,1)} custom-call(bf16[4,96,1152]{2,1,0:T(8,128)(2,1)} %tok.1, f32[3,2,1152]{2,1,0:T(2,128)} %bitcast.1, bf16[1152,3456]{1,0:T(8,128)(2,1)} %w_in0.1, bf16[1152,1152]{1,0:T(8,128)(2,1)} %w_out0.1, bf16[1152,3456]{1,0:T(8,128)(2,1)} %w_in1.1, bf16[1152,1152]{1,0:T(8,128)(2,1)} %w_out1.1), custom_call_target="tpu_custom_call" | custom-call | tf_op jit(solution)/shard_map/block_pair/pallas_call | solution.py:422
  68.4 3.2 %reorder.1 = bf16[4,96,1152]{2,1,0:T(8,128)(2,1)} custom-call(bf16[3,8,16,1152]{3,2,1,0:T(8,128)(2,1)} %block_pair.1.back), custom_call_target="tpu_custom_call" | custom-call | tf_op jit(solution)/shard_map/reorder/pallas_call | solution.py:465

commit v9 on v7

--- a/solution.py
+++ b/solution.py
@@ -196,13 +196,14 @@
     arrive(1, 0)
     arrive(2, 0)
     for piece in range(2):
-        along_y(1, piece).wait_send()
         along_y(3, piece).start()
     arrive(1, 1)
     arrive(2, 1)
     project(0, 1, 2, (0,))
     pass_z(0)
     project(0, 1, 2, (1,))
+    arrive(3, 0)
+    arrive(3, 1)
     project(1, 0, 1)
     pl.semaphore_wait(meet_sem.at[0], 3)
     pl.semaphore_signal(meet_sem.at[1], inc=1, device_id=opposite, device_id_type=MESH)
@@ -272,14 +273,11 @@
             give(g, slot).start()
         own_give(g).start()
 
-    early((0, slice(0, 3)), 288)
-    arrive(3, 0)
-    arrive(3, 1)
-    early((1, slice(0, 3)), 288)
     project(0, 3, 1)
+    early((0, slice(0, 4)), 384)
     pass_z(1)
     pass_z(2)
-    early((slice(0, 2), 3), 192)
+    early((1, slice(0, 4)), 384)
     project(1, 1, 2)
     pass_z(3)
     project(1, 3, 1)
@@ -388,6 +386,7 @@
     lax.fori_loop(0, 3, settle, 0)
 
     for piece in range(2):
+        along_y(1, piece).wait_send()
         along_y(2, piece).wait_send()
         along_y(3, piece).wait_send()
         for slot in range(4):

time: 71.6 us -> 71.1 us (level)
  no operation moved by 1% of the time
where the time goes in v9:
time: 71.1 us; the launch traced here: 71 us
  Pallas kernels  70.9 us (100%)
    pallas_call x1, Pallas kernels, shards(): pl.pallas_call(kernel, out_shape=jax.ShapeDtypeStruct((3, 8, 16, D), jnp....  68.5 us
    pallas_call x1, Pallas kernels, shards(): pl.pallas_call(reorder, out_shape=jax.ShapeDtypeStruct((4, 96, D), jnp.bf...  2.46 us

profile of v9, /device:TPU:0, one launch (start us, length us, event | category | flops | bytes accessed | tf_op | source)
XLA Modules:
  0.0 71.0 jit_solution(12100385842042826445)
XLA Ops:
  0.0 68.5 %block_pair.1.back = bf16[3,8,16,1152]{3,2,1,0:T(8,128)(2,1)} custom-call(bf16[4,96,1152]{2,1,0:T(8,128)(2,1)} %tok.1, f32[3,2,1152]{2,1,0:T(2,128)} %bitcast.1, bf16[1152,3456]{1,0:T(8,128)(2,1)} %w_in0.1, bf16[1152,1152]{1,0:T(8,128)(2,1)} %w_out0.1, bf16[1152,3456]{1,0:T(8,128)(2,1)} %w_in1.1, bf16[1152,1152]{1,0:T(8,128)(2,1)} %w_out1.1), custom_call_target="tpu_custom_call" | custom-call | tf_op jit(solution)/shard_map/block_pair/pallas_call | solution.py:423
  68.5 2.5 %reorder.1 = bf16[4,96,1152]{2,1,0:T(8,128)(2,1)} custom-call(bf16[3,8,16,1152]{3,2,1,0:T(8,128)(2,1)} %block_pair.1.back), custom_call_target="tpu_custom_call" | custom-call | tf_op jit(solution)/shard_map/reorder/pallas_call | solution.py:467

commit v10 on v7

--- a/solution.py
+++ b/solution.py
@@ -196,7 +196,6 @@
     arrive(1, 0)
     arrive(2, 0)
     for piece in range(2):
-        along_y(1, piece).wait_send()
         along_y(3, piece).start()
     arrive(1, 1)
     arrive(2, 1)
@@ -272,9 +271,9 @@
             give(g, slot).start()
         own_give(g).start()
 
-    early((0, slice(0, 3)), 288)
     arrive(3, 0)
     arrive(3, 1)
+    early((0, slice(0, 3)), 288)
     early((1, slice(0, 3)), 288)
     project(0, 3, 1)
     pass_z(1)
@@ -388,6 +387,7 @@
     lax.fori_loop(0, 3, settle, 0)
 
     for piece in range(2):
+        along_y(1, piece).wait_send()
         along_y(2, piece).wait_send()
         along_y(3, piece).wait_send()
         for slot in range(4):

time: 71.6 us -> 71 us (level)
  no operation moved by 1% of the time
where the time goes in v10:
time: 71 us; the launch traced here: 70.8 us
  Pallas kernels  70.8 us (100%)
    pallas_call x1, Pallas kernels, shards(): pl.pallas_call(kernel, out_shape=jax.ShapeDtypeStruct((3, 8, 16, D), jnp....  68.4 us
    pallas_call x1, Pallas kernels, shards(): pl.pallas_call(reorder, out_shape=jax.ShapeDtypeStruct((4, 96, D), jnp.bf...  2.46 us

profile of v10, /device:TPU:0, one launch (start us, length us, event | category | flops | bytes accessed | tf_op | source)
XLA Modules:
  0.0 70.8 jit_solution(9558516340818095611)
XLA Ops:
  0.0 68.4 %block_pair.1.back = bf16[3,8,16,1152]{3,2,1,0:T(8,128)(2,1)} custom-call(bf16[4,96,1152]{2,1,0:T(8,128)(2,1)} %tok.1, f32[3,2,1152]{2,1,0:T(2,128)} %bitcast.1, bf16[1152,3456]{1,0:T(8,128)(2,1)} %w_in0.1, bf16[1152,1152]{1,0:T(8,128)(2,1)} %w_out0.1, bf16[1152,3456]{1,0:T(8,128)(2,1)} %w_in1.1, bf16[1152,1152]{1,0:T(8,128)(2,1)} %w_out1.1), custom_call_target="tpu_custom_call" | custom-call | tf_op jit(solution)/shard_map/block_pair/pallas_call | solution.py:424
  68.4 2.5 %reorder.1 = bf16[4,96,1152]{2,1,0:T(8,128)(2,1)} custom-call(bf16[3,8,16,1152]{3,2,1,0:T(8,128)(2,1)} %block_pair.1.back), custom_call_target="tpu_custom_call" | custom-call | tf_op jit(solution)/shard_map/reorder/pallas_call | solution.py:468
